TPU v7x, 32 devices: a whole 2x2x4 slice. The times are simulated.
32 devices in a mesh: groups: 2 (over x), cells: 16 (over z, y, core).
Axes of the slice: x: 2, y: 2, z: 4, core: 2. Of those that a mesh axis runs over, the one named last changes fastest.
Arguments:
- features: float32 [64, 131072], P(None, ('groups', 'cells')), parts along dimension 1, may hold values from -6 to 6
- weights: float32 [131072], P(('groups', 'cells')), parts along dimension 0, may hold values from 0.5 to 2
- scales: float32 [131072], P(('groups', 'cells')), parts along dimension 0, may hold values from 0.5 to 2
- neighbors: int32 [8, 512], P(None, 'cells'), may hold values from -1 to 511, as said below
Outputs:
- log_scales: float32 [131072], P(('groups', 'cells')), parts along dimension 0
There are 2 independent parts, one for each index of `groups`. A program takes and returns all parts, laid end to end along the dimension named above; an argument that names none is the same for every part. Nothing has to cross between parts.
Inputs may be any that keep to these rules, and one draw needn't show every extreme that they name: `neighbors`: for a block of snapshot s < 3 held by position q of its slab of 4 devices, live entries name blocks of snapshot s + 1 held by positions q - 1, q or q + 1 of the next slab; a block named at position q - 1 is among the last (33) // 2 blocks of that device, one named at position q + 1 among its first (33) // 2; slot 0 names the block at the same place in the next snapshot (index + 128); live slots come first, every such block has at least one, the first block of every device has all 8; blocks of snapshot 4 - 1 have none; entries may repeat.
All inputs are finite; a program needn't handle non-finite values.
Results may differ from a plain program's by a relative error of at most 0.0001.
Values sent between devices are 32-bit elements; how exact they have to be, the bound alone decides.
A program may use at most 64 MiB of HBM per device.

v0:
```python
import jax
import jax.numpy as jnp
from jax import lax
from jax.sharding import PartitionSpec as P

S = 4


def from_behind(block, axis, distance):
    devices = range(lax.axis_size(axis))
    route = [(i - distance, i) for i in devices if i - distance in devices]
    return lax.ppermute(block, axis, route)


def fetch_features(features, slab_size):
    pieces = []
    for offset in (-1, 0, 1):
        if offset < 0:
            source = features
        elif offset > 0:
            source = features
        else:
            source = features
        pieces.append(from_behind(source, "cells", -(slab_size + offset)))
    return jnp.concatenate(pieces, axis=1)


def fetch_values(values, slab_size):
    pieces = [from_behind(values, "cells", -(slab_size + offset)) for offset in (-1, 0, 1)]
    return jnp.concatenate(pieces, axis=0)


def send_partials(partial_value, slab_size, own_blocks):
    total = jnp.zeros((own_blocks, partial_value.shape[1]), jnp.float32)
    for which, offset in enumerate((-1, 0, 1)):
        piece = partial_value[which * own_blocks : (which + 1) * own_blocks]
        total = total + from_behind(piece, "cells", slab_size + offset)
    return total


def local(features, weights, scales, neighbors):
    kernel_width = features.shape[0]
    slot_count, own_blocks = neighbors.shape
    block_len = features.shape[1] // own_blocks
    slab_size = lax.axis_size("cells") // S
    my_index = lax.axis_index("cells")
    slab_index = my_index // slab_size
    entropy_epsilon = kernel_width * 0.25
    live_mask = neighbors >= 0
    active_weight = live_mask.astype(jnp.float32)
    safe_ids = jnp.where(live_mask, neighbors, 0)
    target_dev = safe_ids // own_blocks
    local_ids = safe_ids % own_blocks
    side_off = jnp.clip(target_dev - (my_index + slab_size), -1, 1)
    full_ids = (side_off + 1) * own_blocks + local_ids
    feature_ids = side_off * own_blocks + local_ids + own_blocks
    window = fetch_features(features, slab_size)
    window_blocks = window.reshape(kernel_width, own_blocks + 2 * own_blocks, block_len)
    own_feats = features.reshape(kernel_width, own_blocks, block_len)
    own_norms = jnp.sum(own_feats * own_feats, axis=0)
    other_feats = window_blocks[:, feature_ids, :]
    other_norms = jnp.transpose(jnp.sum(other_feats * other_feats, axis=0), (1, 0, 2))
    cross = jnp.einsum("fbi,fkbj->bkij", own_feats, other_feats, precision=lax.Precision.HIGHEST)
    squared_distance = own_norms[:, None, :, None] + other_norms[:, :, None, :] - 2.0 * cross
    local_holdings = (
        jnp.exp(-squared_distance / entropy_epsilon) * active_weight.T[:, :, None, None]
    )

    def current_tiles():
        return local_holdings

    scale_blocks = scales.reshape(own_blocks, block_len)
    beta = jnp.ones((own_blocks, block_len), jnp.float32)
    for sweep_step in range(S - 1):
        tiles = current_tiles()
        values = (scale_blocks * beta).reshape(-1)
        value_window = fetch_values(values, slab_size).reshape(3 * own_blocks, block_len)
        chosen = value_window[full_ids]
        message = jnp.einsum("bkij,kbj->bi", tiles, chosen, precision=lax.Precision.HIGHEST)
        beta = jnp.where(slab_index == S - 1, jnp.ones_like(message), message)
    onehot = (
        full_ids[:, :, None] == jnp.arange(3 * own_blocks, dtype=jnp.int32)[None, None, :]
    ).astype(jnp.float32)
    onehot = onehot * active_weight[:, :, None]
    phi = jnp.ones((own_blocks, block_len), jnp.float32)
    for sweep_step in range(S - 1):
        tiles = current_tiles()
        weighted = scale_blocks * phi
        contrib = jnp.einsum("bkij,bi->kbj", tiles, weighted, precision=lax.Precision.HIGHEST)
        partial_value = jnp.einsum("kbw,kbj->wj", onehot, contrib, precision=lax.Precision.HIGHEST)
        received = send_partials(partial_value, slab_size, own_blocks)
        phi = jnp.where(slab_index == 0, jnp.ones_like(received), received)
    return jnp.log(weights) - jnp.log(phi.reshape(-1)) - jnp.log(beta.reshape(-1))


def solution(mesh):
    placed = (
        P(None, ("groups", "cells")),
        P(("groups", "cells")),
        P(("groups", "cells")),
        P(None, "cells"),
    )
    return jax.shard_map(
        local, mesh=mesh, in_specs=placed, out_specs=P(("groups", "cells")), check_vma=False
    )
```

profile of v0, /device:TPU:1, one launch (start us, length us, event | category | flops | bytes accessed | tf_op | source)
XLA Modules:
  0.0 259.0 jit_solution(7927702706400792040)
XLA Ops:
  1.3 1.3 collective-permute-start.1
  8.1 2.4 copy.35
  10.6 1.3 multiply_reduce_fusion.1
  11.9 17.5 %collective-permute-done.2 = f32[64,4096]{1,0:T(8,128)S(1)} collective-permute-done((f32[64,4096]{1,0:T(8,128)}, f32[64,4096]{1,0:T(8,128)S(1)}, u32[]{:S(2)}, u32[]{:S(2)}) %collective-permute-start.2) | collective-permute-done | bytes 1048608 | tf_op jit(solution)/shard_map/ppermute | solution.py:12
  30.8 28.4 %collective-permute-done.1 = f32[64,4096]{1,0:T(8,128)S(1)} collective-permute-done((f32[64,4096]{1,0:T(8,128)}, f32[64,4096]{1,0:T(8,128)S(1)}, u32[]{:S(2)}, u32[]{:S(2)}) %collective-permute-start.1) | collective-permute-done | bytes 1048608 | tf_op jit(solution)/shard_map/ppermute | solution.py:12
  60.1 3.5 %collective-permute-done = f32[64,4096]{1,0:T(8,128)} collective-permute-done((f32[64,4096]{1,0:T(8,128)}, f32[64,4096]{1,0:T(8,128)}, u32[]{:S(2)}, u32[]{:S(2)}) %collective-permute-start) | collective-permute-done | bytes 1048608 | tf_op jit(solution)/shard_map/ppermute | solution.py:12
  63.7 2.3 copy_bitcast_fusion
  66.0 4.4 %gather_fusion = f32[256,64,128]{2,1,0:T(8,128)} fusion(f32[64,96,128]{2,0,1:T(8,128)S(1)} %copy_bitcast_fusion, s32[1024]{0:T(1024)S(1)} %pad_clamp_fusion.1), kind=kCustom, calls=%fused_computation | custom fusion | bytes 16778240 | tf_op jit(solution)/shard_map/gather | solution.py:61
  70.4 4.9 %multiply_reduce_fusion = f32[8,32,128]{2,1,0:T(8,128)S(1)} fusion(f32[64,8,32,128]{3,0,2,1:T(8,128)} %bitcast.114), kind=kLoop, calls=%fused_computation.10 | loop fusion | flops 4161536 | bytes 8519680 | tf_op jit(solution)/shard_map/reduce_sum | solution.py:62
  75.4 33.2 %fusion.3 = f32[32,8,128,128]{2,3,1,0:T(8,128)S(1)} fusion(f32[64,8,32,128]{3,0,2,1:T(8,128)} %bitcast.115, f32[32,8]{1,0:T(8,128)S(1)} %copy.18, f32[32,8,128]{2,1,0:T(8,128)S(1)} %copy.15, f32[32,128]{1,0:T(8,128)S(1)} %bitcast.128, f32[64,32,128,1]{2,1,0,3:T(8,128)} %bitcast.117), kind=kOutput, calls=%fused_computation.8 | convolution fusion | flops 3246391296 | bytes 26362880 | tf_op jit(solution)/shard_map/fbi,fkbj->bkij/dot_general | solution.py:63
  108.7 5.7 %copy-done = f32[32,8,128,128]{2,3,1,0:T(8,128)} copy-done((f32[32,8,128,128]{2,3,1,0:T(8,128)}, f32[32,8,128,128]{2,3,1,0:T(8,128)S(1)}, u32[]{:S(2)}) %copy-start) | copy-done | bytes 16777240
  114.4 14.8 %fusion.43 = f32[32,1,8,128]{3,1,2,0:T(1,128)S(1)} fusion(f32[32,8,128,128]{2,3,1,0:T(8,128)S(1)} %fusion.3, f32[32,128,1,1]{1,2,3,0:T(1,128)S(1)} %bitcast.122), kind=kOutput, calls=%fused_computation.78 | convolution fusion | flops 50331648 | bytes 16924672 | tf_op jit(solution)/shard_map/bkij,bi->kbj/dot_general | solution.py:89
  129.7 25.0 %collective-permute-start.5 = (f32[32,128]{1,0:T(8,128)S(1)}, f32[32,128]{1,0:T(8,128)S(1)}, u32[]{:S(2)}, u32[]{:S(2)}) collective-permute-start(f32[32,128]{1,0:T(8,128)S(1)} %get-tuple-element.14), channel_id=1, source_target_pairs={{0,5},{1,6},{2,7},{3,8},{4,9},{5,10},{6,11},{7,12},{8,13},{9,14},{... | collective-permute-start | bytes 49160 | tf_op jit(solution)/shard_map/ppermute | solution.py:12
  156.0 2.4 collective-permute-start.4
  159.3 17.1 %fusion.44 = f32[32,1,8,128]{3,1,2,0:T(1,128)S(1)} fusion(f32[32,128,1,1]{1,2,3,0:T(1,128)S(1)} %bitcast.124, f32[32,8,128,128]{2,3,1,0:T(8,128)} %copy-done), kind=kOutput, calls=%fused_computation.79 | convolution fusion | flops 50331648 | bytes 16924672 | tf_op jit(solution)/shard_map/bkij,bi->kbj/dot_general | solution.py:89
  176.9 4.3 %collective-permute-start.8 = (f32[32,128]{1,0:T(8,128)S(1)}, f32[32,128]{1,0:T(8,128)S(1)}, u32[]{:S(2)}, u32[]{:S(2)}) collective-permute-start(f32[32,128]{1,0:T(8,128)S(1)} %get-tuple-element.11), channel_id=1, source_target_pairs={{0,5},{1,6},{2,7},{3,8},{4,9},{5,10},{6,11},{7,12},{8,13},{9,14},{... | collective-permute-start | bytes 49160 | tf_op jit(solution)/shard_map/ppermute | solution.py:12
  182.5 2.1 collective-permute-start.7
  184.7 9.5 %fusion.16 = f32[32,1,128,1]{2,1,3,0:T(1,128)S(1)} fusion(f32[32,8,128,128]{2,3,1,0:T(8,128)S(1)} %bitcast.113, f32[8,32,128,1]{2,1,0,3:T(8,128)S(1)} %bitcast.118), kind=kOutput, calls=%fused_computation.28 | convolution fusion | flops 50331648 | bytes 16924672 | tf_op jit(solution)/shard_map/bkij,kbj->bi/dot_general | solution.py:79
  198.2 14.7 %fusion.45 = f32[32,1,8,128]{3,1,2,0:T(1,128)S(1)} fusion(f32[32,128,1,1]{1,2,3,0:T(1,128)S(1)} %bitcast.123, f32[32,8,128,128]{2,3,1,0:T(8,128)S(1)} %bitcast.113), kind=kOutput, calls=%fused_computation.80 | convolution fusion | flops 50331648 | bytes 16924672 | tf_op jit(solution)/shard_map/bkij,bi->kbj/dot_general | solution.py:89
  214.2 11.5 %fusion.14 = f32[32,1,128,1]{2,1,3,0:T(1,128)S(1)} fusion(f32[32,8,128,128]{2,3,1,0:T(8,128)} %copy-done, f32[8,32,128,1]{2,1,0,3:T(8,128)S(1)} %bitcast.120), kind=kOutput, calls=%fused_computation.26 | convolution fusion | flops 50331648 | bytes 16924672 | tf_op jit(solution)/shard_map/bkij,kbj->bi/dot_general | solution.py:79
  229.6 8.3 %collective-permute-start.11 = (f32[32,128]{1,0:T(8,128)S(1)}, f32[32,128]{1,0:T(8,128)S(1)}, u32[]{:S(2)}, u32[]{:S(2)}) collective-permute-start(f32[32,128]{1,0:T(8,128)S(1)} %get-tuple-element.8), channel_id=1, source_target_pairs={{0,5},{1,6},{2,7},{3,8},{4,9},{5,10},{6,11},{7,12},{8,13},{9,14},{... | collective-permute-start | bytes 49160 | tf_op jit(solution)/shard_map/ppermute | solution.py:12
  237.9 3.6 %collective-permute-start.9 = (f32[32,128]{1,0:T(8,128)S(1)}, f32[32,128]{1,0:T(8,128)S(1)}, u32[]{:S(2)}, u32[]{:S(2)}) collective-permute-start(f32[32,128]{1,0:T(8,128)S(1)} %get-tuple-element.9), channel_id=1, source_target_pairs={{0,3},{1,4},{2,5},{3,6},{4,7},{5,8},{6,9},{7,10},{8,11},{9,12},{10... | collective-permute-start | bytes 49160 | tf_op jit(solution)/shard_map/ppermute | solution.py:12
  241.5 4.5 %collective-permute-start.10 = (f32[32,128]{1,0:T(8,128)S(1)}, f32[32,128]{1,0:T(8,128)S(1)}, u32[]{:S(2)}, u32[]{:S(2)}) collective-permute-start(f32[32,128]{1,0:T(8,128)S(1)} %get-tuple-element.7), channel_id=1, source_target_pairs={{0,4},{1,5},{2,6},{3,7},{4,8},{5,9},{6,10},{7,11},{8,12},{9,13},{1... | collective-permute-start | bytes 49160 | tf_op jit(solution)/shard_map/ppermute | solution.py:12
  246.9 11.5 %fusion.12 = f32[32,1,128,1]{2,1,3,0:T(1,128)S(1)} fusion(f32[32,8,128,128]{2,3,1,0:T(8,128)} %copy-done, f32[8,32,128,1]{2,1,0,3:T(8,128)S(1)} %bitcast.119), kind=kOutput, calls=%fused_computation.24 | convolution fusion | flops 50331648 | bytes 16924672 | tf_op jit(solution)/shard_map/bkij,kbj->bi/dot_general | solution.py:79
  (73 shorter events, 24.0 us)
Async XLA Ops:
  0.0 29.5 %collective-permute-start.2 = (f32[64,4096]{1,0:T(8,128)}, f32[64,4096]{1,0:T(8,128)S(1)}, u32[]{:S(2)}, u32[]{:S(2)}) collective-permute-start(f32[64,4096]{1,0:T(8,128)} %param.4), channel_id=1, source_target_pairs={{5,0},{6,1},{7,2},{8,3},{9,4},{10,5},{11,6},{12,7},{13,8},{14,9},{... | collective-permute-start | bytes 3145736 | tf_op jit(solution)/shard_map/ppermute | solution.py:12
  1.3 57.8 %collective-permute-start.1 = (f32[64,4096]{1,0:T(8,128)}, f32[64,4096]{1,0:T(8,128)S(1)}, u32[]{:S(2)}, u32[]{:S(2)}) collective-permute-start(f32[64,4096]{1,0:T(8,128)} %param.4), channel_id=1, source_target_pairs={{4,0},{5,1},{6,2},{7,3},{8,4},{9,5},{10,6},{11,7},{12,8},{13,9},{1... | collective-permute-start | bytes 3145736 | tf_op jit(solution)/shard_map/ppermute | solution.py:12
  2.6 61.1 %collective-permute-start = (f32[64,4096]{1,0:T(8,128)}, f32[64,4096]{1,0:T(8,128)}, u32[]{:S(2)}, u32[]{:S(2)}) collective-permute-start(f32[64,4096]{1,0:T(8,128)} %param.4), channel_id=1, source_target_pairs={{3,0},{4,1},{5,2},{6,3},{7,4},{8,5},{9,6},{10,7},{11,8},{12,9},{13... | collective-permute-start | bytes 3145736 | tf_op jit(solution)/shard_map/ppermute | solution.py:12
  3.9 152.1 %collective-permute-start.14 = (f32[4096]{0:T(1024)}, f32[4096]{0:T(1024)S(1)}, u32[]{:S(2)}, u32[]{:S(2)}) collective-permute-start(f32[4096]{0:T(1024)} %param.6), channel_id=1, source_target_pairs={{5,0},{6,1},{7,2},{8,3},{9,4},{10,5},{11,6},{12,7},{13,8},{14,9},{... | collective-permute-start | bytes 49160 | tf_op jit(solution)/shard_map/ppermute | solution.py:12
  5.2 153.3 %collective-permute-start.13 = (f32[4096]{0:T(1024)}, f32[4096]{0:T(1024)S(1)}, u32[]{:S(2)}, u32[]{:S(2)}) collective-permute-start(f32[4096]{0:T(1024)} %param.6), channel_id=1, source_target_pairs={{4,0},{5,1},{6,2},{7,3},{8,4},{9,5},{10,6},{11,7},{12,8},{13,9},{1... | collective-permute-start | bytes 49160 | tf_op jit(solution)/shard_map/ppermute | solution.py:12
  29.5 29.7 %copy-start.1 = (f32[64,4096]{1,0:T(8,128)}, f32[64,4096]{1,0:T(8,128)S(1)}, u32[]{:S(2)}) copy-start(f32[64,4096]{1,0:T(8,128)S(1)} %collective-permute-done.2) | copy-start | bytes 3145732
  29.5 129.0 %collective-permute-start.12 = (f32[4096]{0:T(1024)}, f32[4096]{0:T(1024)S(1)}, u32[]{:S(2)}, u32[]{:S(2)}) collective-permute-start(f32[4096]{0:T(1024)} %param.6), channel_id=1, source_target_pairs={{3,0},{4,1},{5,2},{6,3},{7,4},{8,5},{9,6},{10,7},{11,8},{12,9},{13... | collective-permute-start | bytes 49160 | tf_op jit(solution)/shard_map/ppermute | solution.py:12
  75.4 39.0 %copy-start.3 = (f32[4096]{0:T(1024)S(1)}, f32[4096]{0:T(1024)}, u32[]{:S(2)}) copy-start(f32[4096]{0:T(1024)} %param.6) | copy-start | bytes 49156
  129.7 29.5 %collective-permute-start.5 = (f32[32,128]{1,0:T(8,128)S(1)}, f32[32,128]{1,0:T(8,128)S(1)}, u32[]{:S(2)}, u32[]{:S(2)}) collective-permute-start(f32[32,128]{1,0:T(8,128)S(1)} %get-tuple-element.14), channel_id=1, source_target_pairs={{0,5},{1,6},{2,7},{3,8},{4,9},{5,10},{6,11},{7,12},{8,13},{9,14},{... | collective-permute-start | bytes 49160 | tf_op jit(solution)/shard_map/ppermute | solution.py:12
  154.7 4.5 %collective-permute-start.3 = (f32[32,128]{1,0:T(8,128)S(1)}, f32[32,128]{1,0:T(8,128)S(1)}, u32[]{:S(2)}, u32[]{:S(2)}) collective-permute-start(f32[32,128]{1,0:T(8,128)S(1)} %get-tuple-element.15), channel_id=1, source_target_pairs={{0,3},{1,4},{2,5},{3,6},{4,7},{5,8},{6,9},{7,10},{8,11},{9,12},{10... | collective-permute-start | bytes 49160 | tf_op jit(solution)/shard_map/ppermute | solution.py:12
  156.0 3.3 %collective-permute-start.4 = (f32[32,128]{1,0:T(8,128)S(1)}, f32[32,128]{1,0:T(8,128)S(1)}, u32[]{:S(2)}, u32[]{:S(2)}) collective-permute-start(f32[32,128]{1,0:T(8,128)S(1)} %get-tuple-element.13), channel_id=1, source_target_pairs={{0,4},{1,5},{2,6},{3,7},{4,8},{5,9},{6,10},{7,11},{8,12},{9,13},{1... | collective-permute-start | bytes 49160 | tf_op jit(solution)/shard_map/ppermute | solution.py:12
  176.9 17.3 %collective-permute-start.8 = (f32[32,128]{1,0:T(8,128)S(1)}, f32[32,128]{1,0:T(8,128)S(1)}, u32[]{:S(2)}, u32[]{:S(2)}) collective-permute-start(f32[32,128]{1,0:T(8,128)S(1)} %get-tuple-element.11), channel_id=1, source_target_pairs={{0,5},{1,6},{2,7},{3,8},{4,9},{5,10},{6,11},{7,12},{8,13},{9,14},{... | collective-permute-start | bytes 49160 | tf_op jit(solution)/shard_map/ppermute | solution.py:12
  181.2 13.0 %collective-permute-start.6 = (f32[32,128]{1,0:T(8,128)S(1)}, f32[32,128]{1,0:T(8,128)S(1)}, u32[]{:S(2)}, u32[]{:S(2)}) collective-permute-start(f32[32,128]{1,0:T(8,128)S(1)} %get-tuple-element.12), channel_id=1, source_target_pairs={{0,3},{1,4},{2,5},{3,6},{4,7},{5,8},{6,9},{7,10},{8,11},{9,12},{10... | collective-permute-start | bytes 49160 | tf_op jit(solution)/shard_map/ppermute | solution.py:12
  182.5 11.7 %collective-permute-start.7 = (f32[32,128]{1,0:T(8,128)S(1)}, f32[32,128]{1,0:T(8,128)S(1)}, u32[]{:S(2)}, u32[]{:S(2)}) collective-permute-start(f32[32,128]{1,0:T(8,128)S(1)} %get-tuple-element.10), channel_id=1, source_target_pairs={{0,4},{1,5},{2,6},{3,7},{4,8},{5,9},{6,10},{7,11},{8,12},{9,13},{1... | collective-permute-start | bytes 49160 | tf_op jit(solution)/shard_map/ppermute | solution.py:12
  194.3 19.1 %collective-permute-start.17 = (f32[4096]{0:T(1024)S(1)}, f32[4096]{0:T(1024)S(1)}, u32[]{:S(2)}, u32[]{:S(2)}) collective-permute-start(f32[4096]{0:T(1024)S(1)} %get-tuple-element.17), channel_id=1, source_target_pairs={{5,0},{6,1},{7,2},{8,3},{9,4},{10,5},{11,6},{12,7},{13,8},{14,9},{... | collective-permute-start | bytes 49160 | tf_op jit(solution)/shard_map/ppermute | solution.py:12
  195.6 17.8 %collective-permute-start.16 = (f32[4096]{0:T(1024)S(1)}, f32[4096]{0:T(1024)S(1)}, u32[]{:S(2)}, u32[]{:S(2)}) collective-permute-start(f32[4096]{0:T(1024)S(1)} %get-tuple-element.17), channel_id=1, source_target_pairs={{4,0},{5,1},{6,2},{7,3},{8,4},{9,5},{10,6},{11,7},{12,8},{13,9},{1... | collective-permute-start | bytes 49160 | tf_op jit(solution)/shard_map/ppermute | solution.py:12
  196.9 16.6 %collective-permute-start.15 = (f32[4096]{0:T(1024)S(1)}, f32[4096]{0:T(1024)S(1)}, u32[]{:S(2)}, u32[]{:S(2)}) collective-permute-start(f32[4096]{0:T(1024)S(1)} %get-tuple-element.17), channel_id=1, source_target_pairs={{3,0},{4,1},{5,2},{6,3},{7,4},{8,5},{9,6},{10,7},{11,8},{12,9},{13... | collective-permute-start | bytes 49160 | tf_op jit(solution)/shard_map/ppermute | solution.py:12
  225.6 32.7 %copy-start.4 = (f32[4096]{0:T(1024)S(1)}, f32[4096]{0:T(1024)}, u32[]{:S(2)}) copy-start(f32[4096]{0:T(1024)} %param.5) | copy-start | bytes 49156
  225.7 15.9 %collective-permute-start.20 = (f32[4096]{0:T(1024)S(1)}, f32[4096]{0:T(1024)S(1)}, u32[]{:S(2)}, u32[]{:S(2)}) collective-permute-start(f32[4096]{0:T(1024)S(1)} %fusion.30), channel_id=1, source_target_pairs={{5,0},{6,1},{7,2},{8,3},{9,4},{10,5},{11,6},{12,7},{13,8},{14,9},{... | collective-permute-start | bytes 49160 | tf_op jit(solution)/shard_map/ppermute | solution.py:12
  227.0 19.1 %collective-permute-start.19 = (f32[4096]{0:T(1024)S(1)}, f32[4096]{0:T(1024)S(1)}, u32[]{:S(2)}, u32[]{:S(2)}) collective-permute-start(f32[4096]{0:T(1024)S(1)} %fusion.30), channel_id=1, source_target_pairs={{4,0},{5,1},{6,2},{7,3},{8,4},{9,5},{10,6},{11,7},{12,8},{13,9},{1... | collective-permute-start | bytes 49160 | tf_op jit(solution)/shard_map/ppermute | solution.py:12
  228.3 17.8 %collective-permute-start.18 = (f32[4096]{0:T(1024)S(1)}, f32[4096]{0:T(1024)S(1)}, u32[]{:S(2)}, u32[]{:S(2)}) collective-permute-start(f32[4096]{0:T(1024)S(1)} %fusion.30), channel_id=1, source_target_pairs={{3,0},{4,1},{5,2},{6,3},{7,4},{8,5},{9,6},{10,7},{11,8},{12,9},{13... | collective-permute-start | bytes 49160 | tf_op jit(solution)/shard_map/ppermute | solution.py:12
  229.6 28.8 %collective-permute-start.11 = (f32[32,128]{1,0:T(8,128)S(1)}, f32[32,128]{1,0:T(8,128)S(1)}, u32[]{:S(2)}, u32[]{:S(2)}) collective-permute-start(f32[32,128]{1,0:T(8,128)S(1)} %get-tuple-element.8), channel_id=1, source_target_pairs={{0,5},{1,6},{2,7},{3,8},{4,9},{5,10},{6,11},{7,12},{8,13},{9,14},{... | collective-permute-start | bytes 49160 | tf_op jit(solution)/shard_map/ppermute | solution.py:12
  237.9 20.4 %collective-permute-start.9 = (f32[32,128]{1,0:T(8,128)S(1)}, f32[32,128]{1,0:T(8,128)S(1)}, u32[]{:S(2)}, u32[]{:S(2)}) collective-permute-start(f32[32,128]{1,0:T(8,128)S(1)} %get-tuple-element.9), channel_id=1, source_target_pairs={{0,3},{1,4},{2,5},{3,6},{4,7},{5,8},{6,9},{7,10},{8,11},{9,12},{10... | collective-permute-start | bytes 49160 | tf_op jit(solution)/shard_map/ppermute | solution.py:12
  241.5 16.8 %collective-permute-start.10 = (f32[32,128]{1,0:T(8,128)S(1)}, f32[32,128]{1,0:T(8,128)S(1)}, u32[]{:S(2)}, u32[]{:S(2)}) collective-permute-start(f32[32,128]{1,0:T(8,128)S(1)} %get-tuple-element.7), channel_id=1, source_target_pairs={{0,4},{1,5},{2,6},{3,7},{4,8},{5,9},{6,10},{7,11},{8,12},{9,13},{1... | collective-permute-start | bytes 49160 | tf_op jit(solution)/shard_map/ppermute | solution.py:12
  (6 other events, 108.3 us)
where the time goes:
time: 260 us; the launch traced here: 259 us
  matrix products  114 us (44%)
  starting transfers between devices  68.4 us (26%)
  waiting for transfers between devices  49.6 us (19%)
  local copies, waits for them, and re-layouts  16.2 us (6%)
  other arithmetic  10.6 us (4%)
    ppermute x21, starting transfers between devices, from_behind(): return lax.ppermute(block, axis, route)  68.4 us
    ppermute x21, waiting for transfers between devices, from_behind(): return lax.ppermute(block, axis, route)  49.6 us
    dot_general x3, matrix products, local(): jnp.einsum('bkij,bi->kbj', tiles, weighted, precision=lax.Precision.HIGHEST)  46.6 us
    dot_general x1, matrix products, local(): jnp.einsum('fbi,fkbj->bkij', own_feats, other_feats, precision=lax.Precis...  33.2 us
    dot_general x3, matrix products, local(): jnp.einsum('bkij,kbj->bi', tiles, chosen, precision=lax.Precision.HIGHEST)  32.4 us
    unnamed x19, local copies, waits for them, and re-layouts  9.22 us
  transfers between devices with their start and end apart: 21, of which 4 were waited for; matrix products, arithmetic and copies ran while one was open for 40% of the time, Pallas kernels for 0%

commit v1 on v0

v1 whole, which is shorter than its diff:
```python
import functools
import jax
import jax.numpy as jnp
from jax import lax
from jax.experimental import pallas as pl
from jax.experimental.pallas import tpu as pltpu
from jax.sharding import PartitionSpec as P

S = 4
LOG2E = 1.4426950408889634


def from_next(block, slab, offset):
    n = lax.axis_size("cells")
    route = [
        (i + slab + offset, i)
        for i in range(n - slab)
        if 0 <= i % slab + offset < slab
    ]
    return lax.ppermute(block, "cells", route)


def to_next(block, slab, offset):
    n = lax.axis_size("cells")
    route = [
        (i, i + slab + offset)
        for i in range(n - slab)
        if 0 <= i % slab + offset < slab
    ]
    return lax.ppermute(block, "cells", route)


def split(x):
    hi = x.astype(jnp.bfloat16)
    lo = (x - hi.astype(jnp.float32)).astype(jnp.bfloat16)
    return hi, lo


def stacked(x, eps, own):
    norm = jnp.sum(x * x, axis=0, keepdims=True) * (-LOG2E / eps)
    a = norm.astype(jnp.bfloat16).astype(jnp.float32)
    b = (norm - a).astype(jnp.bfloat16).astype(jnp.float32)
    c = norm - a - b
    row = lax.broadcasted_iota(jnp.int32, (16, x.shape[1]), 0)
    if not own:
        row = row - 3
    tail = jnp.where(row == 0, a, jnp.where(row == 1, b, jnp.where(row == 2, c, 0.0)))
    ones = (row >= 3) & (row < 6) if own else (row < 0)
    tail = jnp.where(ones, 1.0, tail).astype(jnp.bfloat16)
    hi, lo = split(x * (2.0 * LOG2E / eps) if own else x)
    parts = [hi, lo, hi, tail] if own else [hi, hi, lo, tail]
    return jnp.concatenate(parts, axis=0)


def sweep_block(b, slots, ids, live, tile, values, weighted, message, partial):
    blk = message.shape[1]
    column = jnp.broadcast_to(weighted[pl.ds(b, 1), :], (blk, blk)).T
    acc = jnp.zeros((blk, blk), jnp.float32)
    for k in range(slots):
        at = ids[k, b]
        k_tile = tile(k)
        acc = acc + k_tile * values[pl.ds(at, 1), :]
        out = jnp.sum(k_tile * column, axis=0, keepdims=True)
        partial[pl.ds(at, 1), :] += out
    ones = jnp.ones((8, blk), jnp.float32)
    rows = lax.dot_general(
        ones, acc, (((1,), (1,)), ((), ())),
        precision=lax.Precision.HIGHEST, preferred_element_type=jnp.float32,
    )
    message[pl.ds(b, 1), :] = rows[0:1]


def first_kernel(eps, ids, live, below, same, above, feats, values, weighted,
                 tiles, message, partial, stack):
    b = pl.program_id(0)
    slots = ids.shape[0]
    blk = message.shape[1]

    @pl.when(b == 0)
    def _():
        partial[...] = jnp.zeros_like(partial)
        base = 0
        for piece in (below, same, above):
            count = piece.shape[1] // blk

            def prepare(w, _, piece=piece, base=base):
                x = piece[:, pl.ds(pl.multiple_of(w * blk, blk), blk)]
                stack[base + w] = stacked(x, eps, False)
                return 0

            lax.fori_loop(0, count, prepare, 0)
            base += count

    mine = stacked(feats[...], eps, True).T

    def tile(k):
        expo = lax.dot_general(
            mine, stack[ids[k, b]], (((1,), (0,)), ((), ())),
            preferred_element_type=jnp.float32,
        )
        result = jnp.exp2(expo) * live[k, b].astype(jnp.float32)
        tiles[0, :, k * blk : (k + 1) * blk] = result
        return result

    sweep_block(b, slots, ids, live, tile, values, weighted, message, partial)


def next_kernel(ids, live, tiles, values, weighted, message, partial):
    b = pl.program_id(0)
    blk = message.shape[1]

    @pl.when(b == 0)
    def _():
        partial[...] = jnp.zeros_like(partial)

    def tile(k):
        return tiles[0, :, k * blk : (k + 1) * blk]

    sweep_block(b, ids.shape[0], ids, live, tile, values, weighted, message, partial)


def local(features, weights, scales, neighbors):
    dims = features.shape[0]
    slots, own = neighbors.shape
    blk = features.shape[1] // own
    reach = (own + 1) // 2
    wide = own + 2 * reach
    slab = lax.axis_size("cells") // S
    me = lax.axis_index("cells")
    place = me // slab
    eps = dims * 0.25

    live = (neighbors >= 0).astype(jnp.int32)
    first = (me + slab) * own - reach
    ids = jnp.where(neighbors >= 0, neighbors - first, 0)
    ids = jnp.clip(ids, 0, wide - 1)

    same = from_next(features, slab, 0)
    below = from_next(features[:, (own - reach) * blk :], slab, -1)
    above = from_next(features[:, : reach * blk], slab, 1)

    scale = scales.reshape(own, blk)

    def window(values):
        return jnp.concatenate(
            [
                from_next(values[own - reach :], slab, -1),
                from_next(values, slab, 0),
                from_next(values[:reach], slab, 1),
            ],
            axis=0,
        )

    smem = pl.BlockSpec(memory_space=pltpu.SMEM)
    vmem = pl.BlockSpec(memory_space=pltpu.VMEM)
    tile_spec = pl.BlockSpec((1, blk, slots * blk), lambda b: (b, 0, 0))
    rows = jax.ShapeDtypeStruct((own, blk), jnp.float32)
    sums = jax.ShapeDtypeStruct((wide, blk), jnp.float32)
    params = pltpu.CompilerParams(vmem_limit_bytes=32 * 1024 * 1024)

    tiles, message, partial = pl.pallas_call(
        functools.partial(first_kernel, eps),
        grid=(own,),
        in_specs=[smem, smem, vmem, vmem, vmem,
                  pl.BlockSpec((dims, blk), lambda b: (0, b)), vmem, vmem],
        out_specs=[tile_spec, vmem, vmem],
        out_shape=[
            jax.ShapeDtypeStruct((own, blk, slots * blk), jnp.float32), rows, sums,
        ],
        scratch_shapes=[pltpu.VMEM((wide, 3 * dims + 16, blk), jnp.bfloat16)],
        compiler_params=params,
    )(ids, live, below, same, above, features, window(scale), scale)

    def settle(message, partial):
        beta = jnp.where(place == S - 1, 1.0, message)
        total = to_next(partial[reach : reach + own], slab, 0)
        low = to_next(partial[:reach], slab, -1)
        high = to_next(partial[reach + own :], slab, 1)
        total = total.at[own - reach :].add(low)
        total = total.at[:reach].add(high)
        phi = jnp.where(place == 0, 1.0, total)
        return beta, phi

    beta, phi = settle(message, partial)
    for _ in range(S - 2):
        message, partial = pl.pallas_call(
            next_kernel,
            grid=(own,),
            in_specs=[smem, smem, tile_spec, vmem, vmem],
            out_specs=[vmem, vmem],
            out_shape=[rows, sums],
            compiler_params=params,
        )(ids, live, tiles, window(scale * beta), scale * phi)
        beta, phi = settle(message, partial)
    return jnp.log(weights) - jnp.log(phi.reshape(-1)) - jnp.log(beta.reshape(-1))


def solution(mesh):
    placed = (
        P(None, ("groups", "cells")),
        P(("groups", "cells")),
        P(("groups", "cells")),
        P(None, "cells"),
    )
    return jax.shard_map(
        local, mesh=mesh, in_specs=placed, out_specs=P(("groups", "cells")), check_vma=False
    )
```

time: 260 us -> 162 us (0.62)
  matrix products: 114 us -> 0 us
  Pallas kernels: 0 us -> 41.6 us
  starting transfers between devices: 68.4 us -> 49.7 us
  other arithmetic: 10.6 us -> 2.77 us
    dot_general x10 -> x0, matrix products: 114 us -> none  [the longest x3 46.6 us: local(): jnp.einsum('bkij,bi->kbj', tiles, weighted, precision=lax.Precision.HIGHEST)]
    pallas_call x0 -> x3, Pallas kernels: none -> 41.6 us  [the longest x1 24.6 us: local(): pl.pallas_call(functools.partial(first_kernel, eps), grid=(own,), in_spec...]
    ppermute x21, starting transfers between devices: 68.4 us -> 49.7 us  [the longest x9 34.1 us: to_next(): return lax.ppermute(block, 'cells', route)]
    gather x4 -> x0, local copies, waits for them, and re-layouts: 6.6 us -> none  [the longest x1 4.41 us: local(): other_feats = window_blocks[:, feature_ids, :]]
    reduce_sum x2 -> x0, other arithmetic: 6.25 us -> none  [the longest x1 4.92 us: local(): jnp.sum(other_feats * other_feats, axis=0)]
    unnamed x19 -> x12, local copies, waits for them, and re-layouts: 9.22 us -> 13.5 us
  transfers between devices with their start and end apart: 21 -> 21, of which waited for: 4 -> 7; matrix products, arithmetic and copies ran while one was open for 40% -> 2% of each run, Pallas kernels for 0% -> 0%
where the time goes in v1:
time: 162 us; the launch traced here: 161 us
  waiting for transfers between devices  50.9 us (31%)
  starting transfers between devices  49.7 us (31%)
  Pallas kernels  41.6 us (26%)
  local copies, waits for them, and re-layouts  15.5 us (10%)
  other arithmetic  2.77 us (2%)
    ppermute x12, waiting for transfers between devices, from_next(): return lax.ppermute(block, 'cells', route)  48.7 us
    ppermute x9, starting transfers between devices, to_next(): return lax.ppermute(block, 'cells', route)  34.1 us
    pallas_call x1, Pallas kernels, local(): pl.pallas_call(functools.partial(first_kernel, eps), grid=(own,), in_spec...  24.6 us
    pallas_call x2, Pallas kernels, local(): pl.pallas_call(next_kernel, grid=(own,), in_specs=[smem, smem, tile_spec,...  17 us
    ppermute x12, starting transfers between devices, from_next(): return lax.ppermute(block, 'cells', route)  15.6 us
    unnamed x12, local copies, waits for them, and re-layouts  13.5 us
  transfers between devices with their start and end apart: 21, of which 7 were waited for; matrix products, arithmetic and copies ran while one was open for 2% of the time, Pallas kernels for 0%

profile of v1, /device:TPU:1, one launch (start us, length us, event | category | flops | bytes accessed | tf_op | source)
XLA Modules:
  0.0 160.9 jit_solution(8455303799144161253)
XLA Ops:
  0.0 1.4 collective-permute-start.1
  2.7 1.3 collective-permute-start
  4.0 1.3 collective-permute-start.2
  7.3 1.3 collective-permute-start.4
  9.3 36.8 %collective-permute-done.5 = f32[16,128]{1,0:T(8,128)S(1)} collective-permute-done((f32[16,128]{1,0:T(8,128)S(1)}, f32[16,128]{1,0:T(8,128)S(1)}, u32[]{:S(2)}, u32[]{:S(2)}) %collective-permute-start.5) | collective-permute-done | bytes 8224 | tf_op jit(solution)/shard_map/ppermute | solution.py:20
  48.1 3.0 %collective-permute-done.3 = f32[16,128]{1,0:T(8,128)S(1)} collective-permute-done((f32[16,128]{1,0:T(8,128)S(1)}, f32[16,128]{1,0:T(8,128)S(1)}, u32[]{:S(2)}, u32[]{:S(2)}) %collective-permute-start.3) | collective-permute-done | bytes 8224 | tf_op jit(solution)/shard_map/ppermute | solution.py:20
  53.0 24.6 %shard_map.46 = (f32[32,128,1024]{2,1,0:T(8,128)S(1)}, f32[32,128]{1,0:T(8,128)S(1)}, f32[64,128]{1,0:T(8,128)S(1)}) custom-call(s32[8,32]{1,0:T(8,128)S(1)} %select_clamp_fusion.ids, s32[8,32]{1,0:T(8,128)S(1)} %fusion.6.live, f32[64,2048]{1,0:T(8,128)S(1)} %collective-permute-done.below, f32[64,4096]{1,0:T(8,128)S(1)} %collective-permute-done.1.same, ...), custom_call_target="tpu_custom_call" | custom-call | tf_op jit(solution)/shard_map/pallas_call | solution.py:161
  77.7 5.8 %copy-done = f32[32,128,1024]{2,1,0:T(8,128)} copy-done((f32[32,128,1024]{2,1,0:T(8,128)}, f32[32,128,1024]{2,1,0:T(8,128)S(1)}, u32[]{:S(2)}) %copy-start) | copy-done | bytes 16777240
  83.5 3.2 %collective-permute-start.9 = (f32[32,128]{1,0:T(8,128)S(1)}, f32[32,128]{1,0:T(8,128)S(1)}, u32[]{:S(2)}, u32[]{:S(2)}) collective-permute-start(f32[32,128]{1,0:T(8,128)S(1)} %slice.195), channel_id=1, source_target_pairs={{0,4},{1,5},{2,6},{3,7},{4,8},{5,9},{6,10},{7,11},{8,12},{9,13},{1... | collective-permute-start | bytes 49160 | tf_op jit(solution)/shard_map/ppermute | solution.py:30
  86.7 2.3 %collective-permute-start.10 = (f32[16,128]{1,0:T(8,128)S(1)}, f32[16,128]{1,0:T(8,128)S(1)}, u32[]{:S(2)}, u32[]{:S(2)}) collective-permute-start(f32[16,128]{1,0:T(8,128)S(1)} %get-tuple-element.98), channel_id=1, source_target_pairs={{1,4},{2,5},{3,6},{5,8},{6,9},{7,10},{9,12},{10,13},{11,14},{17,20... | collective-permute-start | bytes 24584 | tf_op jit(solution)/shard_map/ppermute | solution.py:30
  89.0 4.1 %collective-permute-start.11 = (f32[16,128]{1,0:T(8,128)S(1)}, f32[16,128]{1,0:T(8,128)S(1)}, u32[]{:S(2)}, u32[]{:S(2)}) collective-permute-start(f32[16,128]{1,0:T(8,128)S(1)} %get-tuple-element.97), channel_id=1, source_target_pairs={{0,5},{1,6},{2,7},{4,9},{5,10},{6,11},{8,13},{9,14},{10,15},{16,21... | collective-permute-start | bytes 24584 | tf_op jit(solution)/shard_map/ppermute | solution.py:30
  95.8 1.3 collective-permute-start.8
  97.1 1.3 collective-permute-start.6
  98.4 4.4 %collective-permute-done.8 = f32[16,128]{1,0:T(8,128)S(1)} collective-permute-done((f32[16,128]{1,0:T(8,128)S(1)}, f32[16,128]{1,0:T(8,128)S(1)}, u32[]{:S(2)}, u32[]{:S(2)}) %collective-permute-start.8) | collective-permute-done | bytes 8224 | tf_op jit(solution)/shard_map/ppermute | solution.py:20
  102.9 5.8 %copy-done.1 = f32[32,128,1024]{2,1,0:T(8,128)S(1)} copy-done((f32[32,128,1024]{2,1,0:T(8,128)S(1)}, f32[32,128,1024]{2,1,0:T(8,128)}, u32[]{:S(2)}) %copy-start.1) | copy-done | bytes 16777240
  108.7 8.5 %shard_map.47 = (f32[32,128]{1,0:T(8,128)S(1)}, f32[64,128]{1,0:T(8,128)S(1)}) custom-call(s32[8,32]{1,0:T(8,128)S(1)} %select_clamp_fusion.ids, s32[8,32]{1,0:T(8,128)S(1)} %fusion.6.live, f32[32,128,1024]{2,1,0:T(8,128)S(1)} %copy-done.1, f32[64,128]{1,0:T(8,128)S(1)} %pad_maximum_fusion.1.values, f32[32,128]{1,0:T(8,128)S(1)} %get-tuple-element.103.weighted), custom_call_target="tpu_custom_call" | custom-call | tf_op jit(solution)/shard_map/pallas_call | solution.py:186
  117.2 3.8 %collective-permute-start.15 = (f32[32,128]{1,0:T(8,128)S(1)}, f32[32,128]{1,0:T(8,128)S(1)}, u32[]{:S(2)}, u32[]{:S(2)}) collective-permute-start(f32[32,128]{1,0:T(8,128)S(1)} %slice.202), channel_id=1, source_target_pairs={{0,4},{1,5},{2,6},{3,7},{4,8},{5,9},{6,10},{7,11},{8,12},{9,13},{1... | collective-permute-start | bytes 49160 | tf_op jit(solution)/shard_map/ppermute | solution.py:30
  121.0 2.2 %collective-permute-start.16 = (f32[16,128]{1,0:T(8,128)S(1)}, f32[16,128]{1,0:T(8,128)S(1)}, u32[]{:S(2)}, u32[]{:S(2)}) collective-permute-start(f32[16,128]{1,0:T(8,128)S(1)} %get-tuple-element.96), channel_id=1, source_target_pairs={{1,4},{2,5},{3,6},{5,8},{6,9},{7,10},{9,12},{10,13},{11,14},{17,20... | collective-permute-start | bytes 24584 | tf_op jit(solution)/shard_map/ppermute | solution.py:30
  123.2 6.2 %collective-permute-start.17 = (f32[16,128]{1,0:T(8,128)S(1)}, f32[16,128]{1,0:T(8,128)S(1)}, u32[]{:S(2)}, u32[]{:S(2)}) collective-permute-start(f32[16,128]{1,0:T(8,128)S(1)} %get-tuple-element.95), channel_id=1, source_target_pairs={{0,5},{1,6},{2,7},{4,9},{5,10},{6,11},{8,13},{9,14},{10,15},{16,21... | collective-permute-start | bytes 24584 | tf_op jit(solution)/shard_map/ppermute | solution.py:30
  134.2 4.4 %collective-permute-done.14 = f32[16,128]{1,0:T(8,128)S(1)} collective-permute-done((f32[16,128]{1,0:T(8,128)S(1)}, f32[16,128]{1,0:T(8,128)S(1)}, u32[]{:S(2)}, u32[]{:S(2)}) %collective-permute-start.14) | collective-permute-done | bytes 8224 | tf_op jit(solution)/shard_map/ppermute | solution.py:20
  138.6 8.5 %shard_map.48 = (f32[32,128]{1,0:T(8,128)S(1)}, f32[64,128]{1,0:T(8,128)S(1)}) custom-call(s32[8,32]{1,0:T(8,128)S(1)} %select_clamp_fusion.ids, s32[8,32]{1,0:T(8,128)S(1)} %fusion.6.live, f32[32,128,1024]{2,1,0:T(8,128)S(1)} %copy-done.1, f32[64,128]{1,0:T(8,128)S(1)} %pad_maximum_fusion.2.values, f32[32,128]{1,0:T(8,128)S(1)} %get-tuple-element.99.weighted), custom_call_target="tpu_custom_call" | custom-call | tf_op jit(solution)/shard_map/pallas_call | solution.py:186
  147.1 3.8 %collective-permute-start.18 = (f32[32,128]{1,0:T(8,128)S(1)}, f32[32,128]{1,0:T(8,128)S(1)}, u32[]{:S(2)}, u32[]{:S(2)}) collective-permute-start(f32[32,128]{1,0:T(8,128)S(1)} %slice.207), channel_id=1, source_target_pairs={{0,4},{1,5},{2,6},{3,7},{4,8},{5,9},{6,10},{7,11},{8,12},{9,13},{1... | collective-permute-start | bytes 49160 | tf_op jit(solution)/shard_map/ppermute | solution.py:30
  151.0 2.2 %collective-permute-start.19 = (f32[16,128]{1,0:T(8,128)S(1)}, f32[16,128]{1,0:T(8,128)S(1)}, u32[]{:S(2)}, u32[]{:S(2)}) collective-permute-start(f32[16,128]{1,0:T(8,128)S(1)} %get-tuple-element.94), channel_id=1, source_target_pairs={{1,4},{2,5},{3,6},{5,8},{6,9},{7,10},{9,12},{10,13},{11,14},{17,20... | collective-permute-start | bytes 24584 | tf_op jit(solution)/shard_map/ppermute | solution.py:30
  153.2 6.3 %collective-permute-start.20 = (f32[16,128]{1,0:T(8,128)S(1)}, f32[16,128]{1,0:T(8,128)S(1)}, u32[]{:S(2)}, u32[]{:S(2)}) collective-permute-start(f32[16,128]{1,0:T(8,128)S(1)} %get-tuple-element.93), channel_id=1, source_target_pairs={{0,5},{1,6},{2,7},{4,9},{5,10},{6,11},{8,13},{9,14},{10,15},{16,21... | collective-permute-start | bytes 24584 | tf_op jit(solution)/shard_map/ppermute | solution.py:30
  (57 shorter events, 16.7 us)
Async XLA Ops:
  0.0 130.3 %copy-start.4 = (f32[4096]{0:T(1024)S(1)}, f32[4096]{0:T(1024)}, u32[]{:S(2)}) copy-start(f32[4096]{0:T(1024)} %param.18) | copy-start | bytes 49156
  0.0 51.1 %collective-permute-start.1 = (f32[64,4096]{1,0:T(8,128)}, f32[64,4096]{1,0:T(8,128)S(1)}, u32[]{:S(2)}, u32[]{:S(2)}) collective-permute-start(f32[64,4096]{1,0:T(8,128)} %feats.1), channel_id=1, source_target_pairs={{4,0},{5,1},{6,2},{7,3},{8,4},{9,5},{10,6},{11,7},{12,8},{13,9},{1... | collective-permute-start | bytes 3145736 | tf_op jit(solution)/shard_map/ppermute | solution.py:20
  2.7 48.4 %collective-permute-start = (f32[64,2048]{1,0:T(8,128)S(1)}, f32[64,2048]{1,0:T(8,128)S(1)}, u32[]{:S(2)}, u32[]{:S(2)}) collective-permute-start(f32[64,2048]{1,0:T(8,128)S(1)} %get-tuple-element.92), channel_id=1, source_target_pairs={{4,1},{5,2},{6,3},{8,5},{9,6},{10,7},{12,9},{13,10},{14,11},{20,17... | collective-permute-start | bytes 1572872 | tf_op jit(solution)/shard_map/ppermute | solution.py:20
  4.0 47.1 %collective-permute-start.2 = (f32[64,2048]{1,0:T(8,128)S(1)}, f32[64,2048]{1,0:T(8,128)S(1)}, u32[]{:S(2)}, u32[]{:S(2)}) collective-permute-start(f32[64,2048]{1,0:T(8,128)S(1)} %get-tuple-element.91), channel_id=1, source_target_pairs={{5,0},{6,1},{7,2},{9,4},{10,5},{11,6},{13,8},{14,9},{15,10},{21,16... | collective-permute-start | bytes 1572872 | tf_op jit(solution)/shard_map/ppermute | solution.py:20
  6.0 40.1 %collective-permute-start.5 = (f32[16,128]{1,0:T(8,128)S(1)}, f32[16,128]{1,0:T(8,128)S(1)}, u32[]{:S(2)}, u32[]{:S(2)}) collective-permute-start(f32[16,128]{1,0:T(8,128)S(1)} %get-tuple-element.108), channel_id=1, source_target_pairs={{5,0},{6,1},{7,2},{9,4},{10,5},{11,6},{13,8},{14,9},{15,10},{21,16... | collective-permute-start | bytes 24584 | tf_op jit(solution)/shard_map/ppermute | solution.py:20
  7.3 43.8 %collective-permute-start.4 = (f32[32,128]{1,0:T(8,128)}, f32[32,128]{1,0:T(8,128)S(1)}, u32[]{:S(2)}, u32[]{:S(2)}) collective-permute-start(f32[32,128]{1,0:T(8,128)} %bitcast.15), channel_id=1, source_target_pairs={{4,0},{5,1},{6,2},{7,3},{8,4},{9,5},{10,6},{11,7},{12,8},{13,9},{1... | collective-permute-start | bytes 49160 | tf_op jit(solution)/shard_map/ppermute | solution.py:20
  46.1 5.0 %collective-permute-start.3 = (f32[16,128]{1,0:T(8,128)S(1)}, f32[16,128]{1,0:T(8,128)S(1)}, u32[]{:S(2)}, u32[]{:S(2)}) collective-permute-start(f32[16,128]{1,0:T(8,128)S(1)} %get-tuple-element.107), channel_id=1, source_target_pairs={{4,1},{5,2},{6,3},{8,5},{9,6},{10,7},{12,9},{13,10},{14,11},{20,17... | collective-permute-start | bytes 24584 | tf_op jit(solution)/shard_map/ppermute | solution.py:20
  77.7 5.8 %copy-start = (f32[32,128,1024]{2,1,0:T(8,128)}, f32[32,128,1024]{2,1,0:T(8,128)S(1)}, u32[]{:S(2)}) copy-start(f32[32,128,1024]{2,1,0:T(8,128)S(1)} %get-tuple-element.84.tiles) | copy-start | bytes 50331652
  83.5 9.6 %collective-permute-start.9 = (f32[32,128]{1,0:T(8,128)S(1)}, f32[32,128]{1,0:T(8,128)S(1)}, u32[]{:S(2)}, u32[]{:S(2)}) collective-permute-start(f32[32,128]{1,0:T(8,128)S(1)} %slice.195), channel_id=1, source_target_pairs={{0,4},{1,5},{2,6},{3,7},{4,8},{5,9},{6,10},{7,11},{8,12},{9,13},{1... | collective-permute-start | bytes 49160 | tf_op jit(solution)/shard_map/ppermute | solution.py:30
  86.7 6.3 %collective-permute-start.10 = (f32[16,128]{1,0:T(8,128)S(1)}, f32[16,128]{1,0:T(8,128)S(1)}, u32[]{:S(2)}, u32[]{:S(2)}) collective-permute-start(f32[16,128]{1,0:T(8,128)S(1)} %get-tuple-element.98), channel_id=1, source_target_pairs={{1,4},{2,5},{3,6},{5,8},{6,9},{7,10},{9,12},{10,13},{11,14},{17,20... | collective-permute-start | bytes 24584 | tf_op jit(solution)/shard_map/ppermute | solution.py:30
  89.0 4.8 %collective-permute-start.11 = (f32[16,128]{1,0:T(8,128)S(1)}, f32[16,128]{1,0:T(8,128)S(1)}, u32[]{:S(2)}, u32[]{:S(2)}) collective-permute-start(f32[16,128]{1,0:T(8,128)S(1)} %get-tuple-element.97), channel_id=1, source_target_pairs={{0,5},{1,6},{2,7},{4,9},{5,10},{6,11},{8,13},{9,14},{10,15},{16,21... | collective-permute-start | bytes 24584 | tf_op jit(solution)/shard_map/ppermute | solution.py:30
  94.5 8.4 %collective-permute-start.7 = (f32[32,128]{1,0:T(8,128)S(1)}, f32[32,128]{1,0:T(8,128)S(1)}, u32[]{:S(2)}, u32[]{:S(2)}) collective-permute-start(f32[32,128]{1,0:T(8,128)S(1)} %get-tuple-element.104), channel_id=1, source_target_pairs={{4,0},{5,1},{6,2},{7,3},{8,4},{9,5},{10,6},{11,7},{12,8},{13,9},{1... | collective-permute-start | bytes 49160 | tf_op jit(solution)/shard_map/ppermute | solution.py:20
  95.8 7.0 %collective-permute-start.8 = (f32[16,128]{1,0:T(8,128)S(1)}, f32[16,128]{1,0:T(8,128)S(1)}, u32[]{:S(2)}, u32[]{:S(2)}) collective-permute-start(f32[16,128]{1,0:T(8,128)S(1)} %get-tuple-element.106), channel_id=1, source_target_pairs={{5,0},{6,1},{7,2},{9,4},{10,5},{11,6},{13,8},{14,9},{15,10},{21,16... | collective-permute-start | bytes 24584 | tf_op jit(solution)/shard_map/ppermute | solution.py:20
  97.1 5.8 %collective-permute-start.6 = (f32[16,128]{1,0:T(8,128)S(1)}, f32[16,128]{1,0:T(8,128)S(1)}, u32[]{:S(2)}, u32[]{:S(2)}) collective-permute-start(f32[16,128]{1,0:T(8,128)S(1)} %get-tuple-element.105), channel_id=1, source_target_pairs={{4,1},{5,2},{6,3},{8,5},{9,6},{10,7},{12,9},{13,10},{14,11},{20,17... | collective-permute-start | bytes 24584 | tf_op jit(solution)/shard_map/ppermute | solution.py:20
  108.7 51.6 %copy-start.5 = (f32[4096]{0:T(1024)S(1)}, f32[4096]{0:T(1024)}, u32[]{:S(2)}) copy-start(f32[4096]{0:T(1024)} %param.17) | copy-start | bytes 49156
  117.2 12.3 %collective-permute-start.15 = (f32[32,128]{1,0:T(8,128)S(1)}, f32[32,128]{1,0:T(8,128)S(1)}, u32[]{:S(2)}, u32[]{:S(2)}) collective-permute-start(f32[32,128]{1,0:T(8,128)S(1)} %slice.202), channel_id=1, source_target_pairs={{0,4},{1,5},{2,6},{3,7},{4,8},{5,9},{6,10},{7,11},{8,12},{9,13},{1... | collective-permute-start | bytes 49160 | tf_op jit(solution)/shard_map/ppermute | solution.py:30
  121.0 8.5 %collective-permute-start.16 = (f32[16,128]{1,0:T(8,128)S(1)}, f32[16,128]{1,0:T(8,128)S(1)}, u32[]{:S(2)}, u32[]{:S(2)}) collective-permute-start(f32[16,128]{1,0:T(8,128)S(1)} %get-tuple-element.96), channel_id=1, source_target_pairs={{1,4},{2,5},{3,6},{5,8},{6,9},{7,10},{9,12},{10,13},{11,14},{17,20... | collective-permute-start | bytes 24584 | tf_op jit(solution)/shard_map/ppermute | solution.py:30
  123.2 7.0 %collective-permute-start.17 = (f32[16,128]{1,0:T(8,128)S(1)}, f32[16,128]{1,0:T(8,128)S(1)}, u32[]{:S(2)}, u32[]{:S(2)}) collective-permute-start(f32[16,128]{1,0:T(8,128)S(1)} %get-tuple-element.95), channel_id=1, source_target_pairs={{0,5},{1,6},{2,7},{4,9},{5,10},{6,11},{8,13},{9,14},{10,15},{16,21... | collective-permute-start | bytes 24584 | tf_op jit(solution)/shard_map/ppermute | solution.py:30
  130.3 8.4 %collective-permute-start.13 = (f32[32,128]{1,0:T(8,128)S(1)}, f32[32,128]{1,0:T(8,128)S(1)}, u32[]{:S(2)}, u32[]{:S(2)}) collective-permute-start(f32[32,128]{1,0:T(8,128)S(1)} %get-tuple-element.100), channel_id=1, source_target_pairs={{4,0},{5,1},{6,2},{7,3},{8,4},{9,5},{10,6},{11,7},{12,8},{13,9},{1... | collective-permute-start | bytes 49160 | tf_op jit(solution)/shard_map/ppermute | solution.py:20
  131.6 7.0 %collective-permute-start.14 = (f32[16,128]{1,0:T(8,128)S(1)}, f32[16,128]{1,0:T(8,128)S(1)}, u32[]{:S(2)}, u32[]{:S(2)}) collective-permute-start(f32[16,128]{1,0:T(8,128)S(1)} %get-tuple-element.102), channel_id=1, source_target_pairs={{5,0},{6,1},{7,2},{9,4},{10,5},{11,6},{13,8},{14,9},{15,10},{21,16... | collective-permute-start | bytes 24584 | tf_op jit(solution)/shard_map/ppermute | solution.py:20
  132.9 5.8 %collective-permute-start.12 = (f32[16,128]{1,0:T(8,128)S(1)}, f32[16,128]{1,0:T(8,128)S(1)}, u32[]{:S(2)}, u32[]{:S(2)}) collective-permute-start(f32[16,128]{1,0:T(8,128)S(1)} %get-tuple-element.101), channel_id=1, source_target_pairs={{4,1},{5,2},{6,3},{8,5},{9,6},{10,7},{12,9},{13,10},{14,11},{20,17... | collective-permute-start | bytes 24584 | tf_op jit(solution)/shard_map/ppermute | solution.py:20
  147.1 12.3 %collective-permute-start.18 = (f32[32,128]{1,0:T(8,128)S(1)}, f32[32,128]{1,0:T(8,128)S(1)}, u32[]{:S(2)}, u32[]{:S(2)}) collective-permute-start(f32[32,128]{1,0:T(8,128)S(1)} %slice.207), channel_id=1, source_target_pairs={{0,4},{1,5},{2,6},{3,7},{4,8},{5,9},{6,10},{7,11},{8,12},{9,13},{1... | collective-permute-start | bytes 49160 | tf_op jit(solution)/shard_map/ppermute | solution.py:30
  151.0 8.5 %collective-permute-start.19 = (f32[16,128]{1,0:T(8,128)S(1)}, f32[16,128]{1,0:T(8,128)S(1)}, u32[]{:S(2)}, u32[]{:S(2)}) collective-permute-start(f32[16,128]{1,0:T(8,128)S(1)} %get-tuple-element.94), channel_id=1, source_target_pairs={{1,4},{2,5},{3,6},{5,8},{6,9},{7,10},{9,12},{10,13},{11,14},{17,20... | collective-permute-start | bytes 24584 | tf_op jit(solution)/shard_map/ppermute | solution.py:30
  153.2 7.0 %collective-permute-start.20 = (f32[16,128]{1,0:T(8,128)S(1)}, f32[16,128]{1,0:T(8,128)S(1)}, u32[]{:S(2)}, u32[]{:S(2)}) collective-permute-start(f32[16,128]{1,0:T(8,128)S(1)} %get-tuple-element.93), channel_id=1, source_target_pairs={{0,5},{1,6},{2,7},{4,9},{5,10},{6,11},{8,13},{9,14},{10,15},{16,21... | collective-permute-start | bytes 24584 | tf_op jit(solution)/shard_map/ppermute | solution.py:30
  (3 other events, 7.7 us)

commit v2 on v1

--- a/solution.py
+++ b/solution.py
@@ -14,16 +14,6 @@
     n = lax.axis_size("cells")
     route = [
         (i + slab + offset, i)
-        for i in range(n - slab)
-        if 0 <= i % slab + offset < slab
-    ]
-    return lax.ppermute(block, "cells", route)
-
-
-def to_next(block, slab, offset):
-    n = lax.axis_size("cells")
-    route = [
-        (i, i + slab + offset)
         for i in range(n - slab)
         if 0 <= i % slab + offset < slab
     ]
@@ -105,18 +95,132 @@
     sweep_block(b, slots, ids, live, tile, values, weighted, message, partial)
 
 
-def next_kernel(ids, live, tiles, values, weighted, message, partial):
-    b = pl.program_id(0)
-    blk = message.shape[1]
-
-    @pl.when(b == 0)
-    def _():
-        partial[...] = jnp.zeros_like(partial)
-
-    def tile(k):
-        return tiles[0, :, k * blk : (k + 1) * blk]
-
-    sweep_block(b, ids.shape[0], ids, live, tile, values, weighted, message, partial)
+def chain_kernel(slab, ids, hot, tiles, scale, message0, partial0, beta, phi,
+                 window, vals, part, same_in, low_in, high_in, contrib,
+                 vsend, vrecv, psend, precv):
+    me = lax.axis_index("cells")
+    place, spot = me // slab, me % slab
+    slots = ids.shape[0]
+    own, blk = scale.shape
+    wide = window.shape[0]
+    reach = (wide - own) // 2
+    inside = (spot > 0, spot >= 0, spot < slab - 1)
+
+    window[...] = jnp.zeros_like(window)
+    low_in[...] = jnp.zeros_like(low_in)
+    high_in[...] = jnp.zeros_like(high_in)
+    vals[...] = scale[...] * message0[...]
+    part[...] = partial0[...]
+
+    barrier = pltpu.get_barrier_semaphore()
+    for near, step in ((place > 0, -slab), (place < S - 1, slab)):
+        for o in (-1, 0, 1):
+            @pl.when(near & inside[o + 1])
+            def _(step=step, o=o):
+                pl.semaphore_signal(
+                    barrier, inc=1, device_id={"cells": me + step + o},
+                    device_id_type=pl.DeviceIdType.MESH,
+                )
+    sides = jnp.where(place > 0, 1, 0) + jnp.where(place < S - 1, 1, 0)
+    near = 1 + jnp.where(inside[0], 1, 0) + jnp.where(inside[2], 1, 0)
+    pl.semaphore_wait(barrier, sides * near)
+
+    def copy(src, dst, send, recv, target):
+        return pltpu.make_async_remote_copy(
+            src_ref=src, dst_ref=dst, send_sem=send, recv_sem=recv,
+            device_id={"cells": target}, device_id_type=pl.DeviceIdType.MESH,
+        )
+
+    value_parts = {
+        -1: (vals.at[pl.ds(0, reach)], window.at[pl.ds(reach + own, reach)]),
+        0: (vals, window.at[pl.ds(reach, own)]),
+        1: (vals.at[pl.ds(own - reach, reach)], window.at[pl.ds(0, reach)]),
+    }
+    sum_parts = {
+        -1: (part.at[pl.ds(0, reach)], low_in),
+        0: (part.at[pl.ds(reach, own)], same_in),
+        1: (part.at[pl.ds(reach + own, reach)], high_in),
+    }
+
+    def value_copy(o):
+        src, dst = value_parts[o]
+        return copy(src, dst, vsend.at[o + 1], vrecv.at[o + 1], me - slab + o)
+
+    def sum_copy(o):
+        src, dst = sum_parts[o]
+        return copy(src, dst, psend.at[o + 1], precv.at[o + 1], me + slab + o)
+
+    def each(cond, make, act, flip=False):
+        for o in (-1, 0, 1):
+            @pl.when(cond & inside[(-o if flip else o) + 1])
+            def _(o=o):
+                getattr(make(o), act)()
+
+    each(place == 2, value_copy, "start")
+    each(place == 0, sum_copy, "start")
+    each(place <= 1, value_copy, "wait_recv", True)
+    each(place >= 1, sum_copy, "wait_recv", True)
+
+    @pl.when(place >= 1)
+    def _():
+        phi[...] = same_in[...]
+        phi[pl.ds(own - reach, reach), :] += low_in[...]
+        phi[pl.ds(0, reach), :] += high_in[...]
+
+    @pl.when(place == 0)
+    def _():
+        phi[...] = jnp.ones_like(phi)
+
+    @pl.when(place == S - 1)
+    def _():
+        beta[...] = jnp.ones_like(beta)
+
+    @pl.when(place == S - 2)
+    def _():
+        beta[...] = message0[...]
+
+    @pl.when(place <= 1)
+    def _():
+        def back(b, _):
+            acc = jnp.zeros((blk, blk), jnp.float32)
+            for k in range(slots):
+                row = window[pl.ds(ids[k, b], 1), :]
+                acc = acc + tiles[b, :, k * blk : (k + 1) * blk] * row
+            rows = lax.dot_general(
+                jnp.ones((8, blk), jnp.float32), acc, (((1,), (1,)), ((), ())),
+                precision=lax.Precision.HIGHEST, preferred_element_type=jnp.float32,
+            )
+            beta[pl.ds(b, 1), :] = rows[0:1]
+            return 0
+
+        lax.fori_loop(0, own, back, 0)
+
+    @pl.when(place == 1)
+    def _():
+        vals[...] = scale[...] * beta[...]
+
+    each(place == 1, value_copy, "start")
+
+    @pl.when((place >= 1) & (place < S - 1))
+    def _():
+        def fore(b, _):
+            weighted = scale[pl.ds(b, 1), :] * phi[pl.ds(b, 1), :]
+            column = jnp.broadcast_to(weighted, (blk, blk)).T
+            for k in range(slots):
+                out = tiles[b, :, k * blk : (k + 1) * blk] * column
+                contrib[b, k : k + 1, :] = jnp.sum(out, axis=0, keepdims=True)
+            return 0
+
+        lax.fori_loop(0, own, fore, 0)
+        part[...] = lax.dot_general(
+            hot[...], contrib[...].reshape(own * slots, blk), (((1,), (0,)), ((), ())),
+            precision=lax.Precision.HIGHEST, preferred_element_type=jnp.float32,
+        )
+
+    late = (place >= 1) & (place < S - 1)
+    each(late, sum_copy, "start")
+    each(late, value_copy, "wait_send")
+    each(place < S - 1, sum_copy, "wait_send")
 
 
 def local(features, weights, scales, neighbors):
@@ -171,27 +275,30 @@
         compiler_params=params,
     )(ids, live, below, same, above, features, window(scale), scale)
 
-    def settle(message, partial):
-        beta = jnp.where(place == S - 1, 1.0, message)
-        total = to_next(partial[reach : reach + own], slab, 0)
-        low = to_next(partial[:reach], slab, -1)
-        high = to_next(partial[reach + own :], slab, 1)
-        total = total.at[own - reach :].add(low)
-        total = total.at[:reach].add(high)
-        phi = jnp.where(place == 0, 1.0, total)
-        return beta, phi
-
-    beta, phi = settle(message, partial)
-    for _ in range(S - 2):
-        message, partial = pl.pallas_call(
-            next_kernel,
-            grid=(own,),
-            in_specs=[smem, smem, tile_spec, vmem, vmem],
-            out_specs=[vmem, vmem],
-            out_shape=[rows, sums],
-            compiler_params=params,
-        )(ids, live, tiles, window(scale * beta), scale * phi)
-        beta, phi = settle(message, partial)
+    at = ids.T.reshape(1, own * slots)
+    hot = (at == jnp.arange(wide, dtype=jnp.int32)[:, None]) & (
+        live.T.reshape(1, own * slots) > 0
+    )
+    sem = pltpu.SemaphoreType.DMA((3,))
+    beta, phi = pl.pallas_call(
+        functools.partial(chain_kernel, slab),
+        in_specs=[smem] + [vmem] * 5,
+        out_specs=[vmem, vmem],
+        out_shape=[rows, rows],
+        scratch_shapes=[
+            pltpu.VMEM((wide, blk), jnp.float32),
+            pltpu.VMEM((own, blk), jnp.float32),
+            pltpu.VMEM((wide, blk), jnp.float32),
+            pltpu.VMEM((own, blk), jnp.float32),
+            pltpu.VMEM((reach, blk), jnp.float32),
+            pltpu.VMEM((reach, blk), jnp.float32),
+            pltpu.VMEM((own, slots, blk), jnp.float32),
+            sem, sem, sem, sem,
+        ],
+        compiler_params=pltpu.CompilerParams(
+            collective_id=0, has_side_effects=True, vmem_limit_bytes=40 * 1024 * 1024
+        ),
+    )(ids, hot.astype(jnp.float32), tiles, scale, message, partial)
     return jnp.log(weights) - jnp.log(phi.reshape(-1)) - jnp.log(beta.reshape(-1))
 
 

time: 162 us -> 114 us (0.70)
  starting transfers between devices: 49.7 us -> 7.86 us
  waiting for transfers between devices: 50.9 us -> 37.5 us
  Pallas kernels: 41.6 us -> 53.3 us
  local copies, waits for them, and re-layouts: 15.5 us -> 10.8 us
    ppermute x9 -> x0, starting transfers between devices: 34.1 us -> none  [to_next(): return lax.ppermute(block, 'cells', route)]
    pallas_call x2 -> x1, Pallas kernels: 17 us -> 28.6 us  [local(): pl.pallas_call(functools.partial(chain_kernel, slab), in_specs=[smem] + [...]
    ppermute x12 -> x6, waiting for transfers between devices: 48.7 us -> 37.5 us  [from_next(): return lax.ppermute(block, 'cells', route)]
    ppermute x12 -> x6, starting transfers between devices: 15.6 us -> 7.86 us  [from_next(): return lax.ppermute(block, 'cells', route)]
    unnamed x12 -> x10, local copies, waits for them, and re-layouts: 13.5 us -> 8.43 us
    ppermute x9 -> x0, waiting for transfers between devices: 2.24 us -> none  [to_next(): return lax.ppermute(block, 'cells', route)]
  transfers between devices with their start and end apart: 21 -> 6, of which waited for: 7 -> 1; matrix products, arithmetic and copies ran while one was open for 2% -> 4% of each run, Pallas kernels for 0% -> 0%
where the time goes in v2:
time: 114 us; the launch traced here: 112 us
  Pallas kernels  53.3 us (47%)
  waiting for transfers between devices  37.5 us (33%)
  local copies, waits for them, and re-layouts  10.8 us (9%)
  starting transfers between devices  7.86 us (7%)
  other arithmetic  2.73 us (2%)
    ppermute x6, waiting for transfers between devices, from_next(): return lax.ppermute(block, 'cells', route)  37.5 us
    pallas_call x1, Pallas kernels, local(): pl.pallas_call(functools.partial(chain_kernel, slab), in_specs=[smem] + [...  28.6 us
    pallas_call x1, Pallas kernels, local(): pl.pallas_call(functools.partial(first_kernel, eps), grid=(own,), in_spec...  24.7 us
    unnamed x10, local copies, waits for them, and re-layouts  8.43 us
    ppermute x6, starting transfers between devices, from_next(): return lax.ppermute(block, 'cells', route)  7.86 us
  transfers between devices with their start and end apart: 6, of which 1 were waited for; matrix products, arithmetic and copies ran while one was open for 4% of the time, Pallas kernels for 0%

profile of v2, /device:TPU:1, one launch (start us, length us, event | category | flops | bytes accessed | tf_op | source)
XLA Modules:
  0.0 112.3 jit_solution(12527453043815417035)
XLA Ops:
  0.0 1.4 %collective-permute-start.4 = (f32[32,128]{1,0:T(8,128)}, f32[32,128]{1,0:T(8,128)S(1)}, u32[]{:S(2)}, u32[]{:S(2)}) collective-permute-start(f32[32,128]{1,0:T(8,128)} %bitcast.15), channel_id=1, source_target_pairs={{4,0},{5,1},{6,2},{7,3},{8,4},{9,5},{10,6},{11,7},{12,8},{13,9},{1... | collective-permute-start | bytes 49160 | tf_op jit(solution)/shard_map/ppermute | solution.py:20
  1.4 0.7 slice_bitcast_fusion.1
  2.1 1.3 %collective-permute-start.3 = (f32[16,128]{1,0:T(8,128)S(1)}, f32[16,128]{1,0:T(8,128)S(1)}, u32[]{:S(2)}, u32[]{:S(2)}) collective-permute-start(f32[16,128]{1,0:T(8,128)S(1)} %get-tuple-element.17), channel_id=1, source_target_pairs={{4,1},{5,2},{6,3},{8,5},{9,6},{10,7},{12,9},{13,10},{14,11},{20,17... | collective-permute-start | bytes 24584 | tf_op jit(solution)/shard_map/ppermute | solution.py:20
  3.4 1.3 %collective-permute-start.1 = (f32[64,4096]{1,0:T(8,128)}, f32[64,4096]{1,0:T(8,128)S(1)}, u32[]{:S(2)}, u32[]{:S(2)}) collective-permute-start(f32[64,4096]{1,0:T(8,128)} %feats.1), channel_id=1, source_target_pairs={{4,0},{5,1},{6,2},{7,3},{8,4},{9,5},{10,6},{11,7},{12,8},{13,9},{1... | collective-permute-start | bytes 3145736 | tf_op jit(solution)/shard_map/ppermute | solution.py:20
  4.7 1.3 %fusion.3 = (f32[64,2048]{1,0:T(8,128)S(1)}, f32[64,2048]{1,0:T(8,128)S(1)}) fusion(f32[64,4096]{1,0:T(8,128)} %feats.1), kind=kLoop, calls=%fused_computation.12 | loop fusion | bytes 2097152 | tf_op jit(solution)/shard_map/slice | solution.py:244
  6.0 1.3 %collective-permute-start = (f32[64,2048]{1,0:T(8,128)S(1)}, f32[64,2048]{1,0:T(8,128)S(1)}, u32[]{:S(2)}, u32[]{:S(2)}) collective-permute-start(f32[64,2048]{1,0:T(8,128)S(1)} %get-tuple-element.16), channel_id=1, source_target_pairs={{4,1},{5,2},{6,3},{8,5},{9,6},{10,7},{12,9},{13,10},{14,11},{20,17... | collective-permute-start | bytes 1572872 | tf_op jit(solution)/shard_map/ppermute | solution.py:20
  7.3 1.3 %collective-permute-start.2 = (f32[64,2048]{1,0:T(8,128)S(1)}, f32[64,2048]{1,0:T(8,128)S(1)}, u32[]{:S(2)}, u32[]{:S(2)}) collective-permute-start(f32[64,2048]{1,0:T(8,128)S(1)} %get-tuple-element.15), channel_id=1, source_target_pairs={{5,0},{6,1},{7,2},{9,4},{10,5},{11,6},{13,8},{14,9},{15,10},{21,16... | collective-permute-start | bytes 1572872 | tf_op jit(solution)/shard_map/ppermute | solution.py:20
  8.6 0.7 fusion.4
  9.3 0.1 copy.5
  9.4 0.1 eq.15
  9.5 0.7 fusion.2
  10.2 0.1 copy.6
  10.3 0.1 gt.17
  10.4 1.3 %collective-permute-start.5 = (f32[16,128]{1,0:T(8,128)S(1)}, f32[16,128]{1,0:T(8,128)S(1)}, u32[]{:S(2)}, u32[]{:S(2)}) collective-permute-start(f32[16,128]{1,0:T(8,128)S(1)} %get-tuple-element.18), channel_id=1, source_target_pairs={{5,0},{6,1},{7,2},{9,4},{10,5},{11,6},{13,8},{14,9},{15,10},{21,16... | collective-permute-start | bytes 24584 | tf_op jit(solution)/shard_map/ppermute | solution.py:20
  11.7 0.7 select_clamp_fusion.ids
  12.4 37.5 %collective-permute-done.5 = f32[16,128]{1,0:T(8,128)S(1)} collective-permute-done((f32[16,128]{1,0:T(8,128)S(1)}, f32[16,128]{1,0:T(8,128)S(1)}, u32[]{:S(2)}, u32[]{:S(2)}) %collective-permute-start.5) | collective-permute-done | bytes 8224 | tf_op jit(solution)/shard_map/ppermute | solution.py:20
  49.9 0.0 copy-start.1
  49.9 1.2 %copy-done.1 = f32[64,4096]{1,0:T(8,128)S(1)} copy-done((f32[64,4096]{1,0:T(8,128)S(1)}, f32[64,4096]{1,0:T(8,128)}, u32[]{:S(2)}) %copy-start.1) | copy-done | bytes 1048600
  51.2 0.7 copy-done.2
  51.9 24.7 %shard_map.46 = (f32[32,128,1024]{2,1,0:T(8,128)S(1)}, f32[32,128]{1,0:T(8,128)S(1)}, f32[64,128]{1,0:T(8,128)S(1)}) custom-call(s32[8,32]{1,0:T(8,128)S(1)} %select_clamp_fusion.ids, s32[8,32]{1,0:T(8,128)S(1)} %get-tuple-element.19.live, f32[64,2048]{1,0:T(8,128)S(1)} %collective-permute-done.below, f32[64,4096]{1,0:T(8,128)S(1)} %collective-permute-done.1.same, ...), custom_call_target="tpu_custom_call" | custom-call | tf_op jit(solution)/shard_map/pallas_call | solution.py:265
  76.6 5.8 %copy-done = f32[32,128,1024]{2,1,0:T(8,128)} copy-done((f32[32,128,1024]{2,1,0:T(8,128)}, f32[32,128,1024]{2,1,0:T(8,128)S(1)}, u32[]{:S(2)}) %copy-start) | copy-done | bytes 16777240
  82.3 0.7 copy-done.3
  83.1 28.6 %shard_map.47 = (f32[32,128]{1,0:T(8,128)S(1)}, f32[32,128]{1,0:T(8,128)S(1)}) custom-call(s32[8,32]{1,0:T(8,128)S(1)} %select_clamp_fusion.ids, f32[64,256]{1,0:T(8,128)S(1)} %fusion.1.hot, f32[32,128,1024]{2,1,0:T(8,128)} %copy-done, f32[32,128]{1,0:T(8,128)S(1)} %bitcast.17, f32[32,128]{1,0:T(8,128)S(1)} %get-tuple-element.11.message0, ...), custom_call_target="tpu_custom_call" | custom-call | tf_op jit(solution)/shard_map/pallas_call | solution.py:283
  111.7 0.6 bitcast_subtract_fusion
  (12 shorter events, 0.0 us)
Async XLA Ops:
  0.0 111.6 %copy-start.4 = (f32[4096]{0:T(1024)S(1)}, f32[4096]{0:T(1024)}, u32[]{:S(2)}) copy-start(f32[4096]{0:T(1024)} %param.5) | copy-start | bytes 49156
  0.0 49.9 %collective-permute-start.4 = (f32[32,128]{1,0:T(8,128)}, f32[32,128]{1,0:T(8,128)S(1)}, u32[]{:S(2)}, u32[]{:S(2)}) collective-permute-start(f32[32,128]{1,0:T(8,128)} %bitcast.15), channel_id=1, source_target_pairs={{4,0},{5,1},{6,2},{7,3},{8,4},{9,5},{10,6},{11,7},{12,8},{13,9},{1... | collective-permute-start | bytes 49160 | tf_op jit(solution)/shard_map/ppermute | solution.py:20
  2.1 8.3 %collective-permute-start.3 = (f32[16,128]{1,0:T(8,128)S(1)}, f32[16,128]{1,0:T(8,128)S(1)}, u32[]{:S(2)}, u32[]{:S(2)}) collective-permute-start(f32[16,128]{1,0:T(8,128)S(1)} %get-tuple-element.17), channel_id=1, source_target_pairs={{4,1},{5,2},{6,3},{8,5},{9,6},{10,7},{12,9},{13,10},{14,11},{20,17... | collective-permute-start | bytes 24584 | tf_op jit(solution)/shard_map/ppermute | solution.py:20
  3.4 46.5 %collective-permute-start.1 = (f32[64,4096]{1,0:T(8,128)}, f32[64,4096]{1,0:T(8,128)S(1)}, u32[]{:S(2)}, u32[]{:S(2)}) collective-permute-start(f32[64,4096]{1,0:T(8,128)} %feats.1), channel_id=1, source_target_pairs={{4,0},{5,1},{6,2},{7,3},{8,4},{9,5},{10,6},{11,7},{12,8},{13,9},{1... | collective-permute-start | bytes 3145736 | tf_op jit(solution)/shard_map/ppermute | solution.py:20
  6.0 43.9 %collective-permute-start = (f32[64,2048]{1,0:T(8,128)S(1)}, f32[64,2048]{1,0:T(8,128)S(1)}, u32[]{:S(2)}, u32[]{:S(2)}) collective-permute-start(f32[64,2048]{1,0:T(8,128)S(1)} %get-tuple-element.16), channel_id=1, source_target_pairs={{4,1},{5,2},{6,3},{8,5},{9,6},{10,7},{12,9},{13,10},{14,11},{20,17... | collective-permute-start | bytes 1572872 | tf_op jit(solution)/shard_map/ppermute | solution.py:20
  7.3 42.6 %collective-permute-start.2 = (f32[64,2048]{1,0:T(8,128)S(1)}, f32[64,2048]{1,0:T(8,128)S(1)}, u32[]{:S(2)}, u32[]{:S(2)}) collective-permute-start(f32[64,2048]{1,0:T(8,128)S(1)} %get-tuple-element.15), channel_id=1, source_target_pairs={{5,0},{6,1},{7,2},{9,4},{10,5},{11,6},{13,8},{14,9},{15,10},{21,16... | collective-permute-start | bytes 1572872 | tf_op jit(solution)/shard_map/ppermute | solution.py:20
  10.4 39.5 %collective-permute-start.5 = (f32[16,128]{1,0:T(8,128)S(1)}, f32[16,128]{1,0:T(8,128)S(1)}, u32[]{:S(2)}, u32[]{:S(2)}) collective-permute-start(f32[16,128]{1,0:T(8,128)S(1)} %get-tuple-element.18), channel_id=1, source_target_pairs={{5,0},{6,1},{7,2},{9,4},{10,5},{11,6},{13,8},{14,9},{15,10},{21,16... | collective-permute-start | bytes 24584 | tf_op jit(solution)/shard_map/ppermute | solution.py:20
  49.9 1.2 %copy-start.1 = (f32[64,4096]{1,0:T(8,128)S(1)}, f32[64,4096]{1,0:T(8,128)}, u32[]{:S(2)}) copy-start(f32[64,4096]{1,0:T(8,128)} %feats.1) | copy-start | bytes 3145732
  51.2 0.7 copy-start.2
  76.6 5.8 %copy-start = (f32[32,128,1024]{2,1,0:T(8,128)}, f32[32,128,1024]{2,1,0:T(8,128)S(1)}, u32[]{:S(2)}) copy-start(f32[32,128,1024]{2,1,0:T(8,128)S(1)} %get-tuple-element.10.tiles) | copy-start | bytes 50331652
  82.3 0.7 copy-start.3

commit v3 on v2

v3 whole, which is shorter than its diff:
```python
import functools
import jax
import jax.numpy as jnp
from jax import lax
from jax.experimental import pallas as pl
from jax.experimental.pallas import tpu as pltpu
from jax.sharding import PartitionSpec as P

S = 4
LOG2E = 1.4426950408889634


def split(x):
    hi = x.astype(jnp.bfloat16)
    lo = (x - hi.astype(jnp.float32)).astype(jnp.bfloat16)
    return hi, lo


def stacked(x, eps, own):
    norm = jnp.sum(x * x, axis=0, keepdims=True) * (-LOG2E / eps)
    a = norm.astype(jnp.bfloat16).astype(jnp.float32)
    b = (norm - a).astype(jnp.bfloat16).astype(jnp.float32)
    c = norm - a - b
    row = lax.broadcasted_iota(jnp.int32, (16, x.shape[1]), 0)
    if not own:
        row = row - 3
    tail = jnp.where(row == 0, a, jnp.where(row == 1, b, jnp.where(row == 2, c, 0.0)))
    ones = (row >= 3) & (row < 6) if own else (row < 0)
    tail = jnp.where(ones, 1.0, tail).astype(jnp.bfloat16)
    hi, lo = split(x * (2.0 * LOG2E / eps) if own else x)
    parts = [hi, lo, hi, tail] if own else [hi, hi, lo, tail]
    return jnp.concatenate(parts, axis=0)


def chain_kernel(slab, eps, ids, live, feats, hot, scale, beta, phi,
                 tiles, fwin, stack,
                 window, vals, part, same_in, low_in, high_in, contrib,
                 fsend, frecv, vsend, vrecv, psend, precv):
    me = lax.axis_index("cells")
    place, spot = me // slab, me % slab
    slots = ids.shape[0]
    own, blk = scale.shape
    wide = window.shape[0]
    reach = (wide - own) // 2
    inside = (spot > 0, spot >= 0, spot < slab - 1)

    window[...] = jnp.zeros_like(window)
    low_in[...] = jnp.zeros_like(low_in)
    high_in[...] = jnp.zeros_like(high_in)
    vals[...] = scale[...]
    edge, middle = reach * blk, own * blk
    fwin[:, :edge] = jnp.zeros((fwin.shape[0], edge), jnp.float32)
    fwin[:, edge + middle :] = jnp.zeros((fwin.shape[0], edge), jnp.float32)

    barrier = pltpu.get_barrier_semaphore()
    for near, step in ((place > 0, -slab), (place < S - 1, slab)):
        for o in (-1, 0, 1):
            @pl.when(near & inside[o + 1])
            def _(step=step, o=o):
                pl.semaphore_signal(
                    barrier, inc=1, device_id={"cells": me + step + o},
                    device_id_type=pl.DeviceIdType.MESH,
                )
    sides = jnp.where(place > 0, 1, 0) + jnp.where(place < S - 1, 1, 0)
    near = 1 + jnp.where(inside[0], 1, 0) + jnp.where(inside[2], 1, 0)
    pl.semaphore_wait(barrier, sides * near)

    def copy(src, dst, send, recv, target):
        return pltpu.make_async_remote_copy(
            src_ref=src, dst_ref=dst, send_sem=send, recv_sem=recv,
            device_id={"cells": target}, device_id_type=pl.DeviceIdType.MESH,
        )

    value_parts = {
        -1: (vals.at[pl.ds(0, reach)], window.at[pl.ds(reach + own, reach)]),
        0: (vals, window.at[pl.ds(reach, own)]),
        1: (vals.at[pl.ds(own - reach, reach)], window.at[pl.ds(0, reach)]),
    }
    sum_parts = {
        -1: (part.at[pl.ds(0, reach)], low_in),
        0: (part.at[pl.ds(reach, own)], same_in),
        1: (part.at[pl.ds(reach + own, reach)], high_in),
    }

    feature_parts = {
        -1: (feats.at[:, pl.ds(0, edge)], fwin.at[:, pl.ds(edge + middle, edge)]),
        0: (feats, fwin.at[:, pl.ds(edge, middle)]),
        1: (feats.at[:, pl.ds(middle - edge, edge)], fwin.at[:, pl.ds(0, edge)]),
    }

    def feature_copy(o):
        src, dst = feature_parts[o]
        return copy(src, dst, fsend.at[o + 1], frecv.at[o + 1], me - slab + o)

    def value_copy(o):
        src, dst = value_parts[o]
        return copy(src, dst, vsend.at[o + 1], vrecv.at[o + 1], me - slab + o)

    def sum_copy(o):
        src, dst = sum_parts[o]
        return copy(src, dst, psend.at[o + 1], precv.at[o + 1], me + slab + o)

    def each(cond, make, act, flip=False):
        for o in (-1, 0, 1):
            @pl.when(cond & inside[(-o if flip else o) + 1])
            def _(o=o):
                getattr(make(o), act)()

    each(place >= 1, feature_copy, "start")
    each(place == S - 1, value_copy, "start")
    has_next = place < S - 1
    each(has_next, feature_copy, "wait_recv", True)

    def lanes(b):
        return pl.ds(pl.multiple_of(b * blk, blk), blk)

    @pl.when(has_next)
    def _():
        def prepare(w, _):
            stack[w] = stacked(fwin[:, lanes(w)], eps, False)
            return 0

        lax.fori_loop(0, wide, prepare, 0)

        def build(b, _):
            mine = stacked(feats[:, lanes(b)], eps, True).T
            for k in range(0, slots, 2):
                theirs = jnp.concatenate(
                    [stack[ids[k, b]], stack[ids[k + 1, b]]], axis=1
                )
                expo = lax.dot_general(
                    mine, theirs, (((1,), (0,)), ((), ())),
                    preferred_element_type=jnp.float32,
                )
                tile = jnp.exp2(expo)
                for i in (0, 1):
                    tiles[b, :, (k + i) * blk : (k + i + 1) * blk] = (
                        tile[:, i * blk : (i + 1) * blk] * live[k + i, b]
                    )
            return 0

        lax.fori_loop(0, own, build, 0)

    def forward(cond):
        @pl.when(cond)
        def _():
            def fore(b, _):
                weighted = scale[pl.ds(b, 1), :] * phi[pl.ds(b, 1), :]
                column = jnp.broadcast_to(weighted, (blk, blk)).T
                for k in range(slots):
                    out = tiles[b, :, k * blk : (k + 1) * blk] * column
                    contrib[b, k : k + 1, :] = jnp.sum(out, axis=0, keepdims=True)
                return 0

            lax.fori_loop(0, own, fore, 0)
            part[...] = lax.dot_general(
                hot[...], contrib[...].reshape(own * slots, blk),
                (((1,), (0,)), ((), ())),
                precision=lax.Precision.HIGHEST, preferred_element_type=jnp.float32,
            )

        each(cond, sum_copy, "start")

    @pl.when(place == 0)
    def _():
        phi[...] = jnp.ones_like(phi)

    @pl.when(place == S - 1)
    def _():
        beta[...] = jnp.ones_like(beta)

    forward(place == 0)
    each(has_next, value_copy, "wait_recv", True)

    @pl.when(has_next)
    def _():
        def back(b, _):
            acc = jnp.zeros((blk, blk), jnp.float32)
            for k in range(slots):
                row = window[pl.ds(ids[k, b], 1), :]
                acc = acc + tiles[b, :, k * blk : (k + 1) * blk] * row
            rows = lax.dot_general(
                jnp.ones((8, blk), jnp.float32), acc, (((1,), (1,)), ((), ())),
                precision=lax.Precision.HIGHEST, preferred_element_type=jnp.float32,
            )
            beta[pl.ds(b, 1), :] = rows[0:1]
            return 0

        lax.fori_loop(0, own, back, 0)
        vals[...] = scale[...] * beta[...]

    each((place >= 1) & has_next, value_copy, "start")
    each(place >= 1, sum_copy, "wait_recv", True)

    @pl.when(place >= 1)
    def _():
        phi[...] = same_in[...]
        phi[pl.ds(own - reach, reach), :] += low_in[...]
        phi[pl.ds(0, reach), :] += high_in[...]

    forward((place >= 1) & has_next)
    each(place >= 1, feature_copy, "wait_send")
    each(place >= 1, value_copy, "wait_send")
    each(has_next, sum_copy, "wait_send")


def local(features, weights, scales, neighbors):
    dims = features.shape[0]
    slots, own = neighbors.shape
    blk = features.shape[1] // own
    reach = (own + 1) // 2
    wide = own + 2 * reach
    slab = lax.axis_size("cells") // S
    me = lax.axis_index("cells")
    eps = dims * 0.25

    live = (neighbors >= 0).astype(jnp.float32)
    first = (me + slab) * own - reach
    ids = jnp.where(neighbors >= 0, neighbors - first, reach)
    ids = jnp.clip(ids, 0, wide - 1)

    scale = scales.reshape(own, blk)
    smem = pl.BlockSpec(memory_space=pltpu.SMEM)
    vmem = pl.BlockSpec(memory_space=pltpu.VMEM)
    rows = jax.ShapeDtypeStruct((own, blk), jnp.float32)
    at = ids.T.reshape(1, own * slots)
    hot = (at == jnp.arange(wide, dtype=jnp.int32)[:, None]) & (
        live.T.reshape(1, own * slots) > 0
    )
    sem = pltpu.SemaphoreType.DMA((3,))
    beta, phi = pl.pallas_call(
        functools.partial(chain_kernel, slab, eps),
        in_specs=[smem] * 2 + [vmem] * 3,
        out_specs=[vmem, vmem],
        out_shape=[rows, rows],
        scratch_shapes=[
            pltpu.VMEM((own, blk, slots * blk), jnp.float32),
            pltpu.VMEM((dims, wide * blk), jnp.float32),
            pltpu.VMEM((wide, 3 * dims + 16, blk), jnp.bfloat16),
            pltpu.VMEM((wide, blk), jnp.float32),
            pltpu.VMEM((own, blk), jnp.float32),
            pltpu.VMEM((wide, blk), jnp.float32),
            pltpu.VMEM((own, blk), jnp.float32),
            pltpu.VMEM((reach, blk), jnp.float32),
            pltpu.VMEM((reach, blk), jnp.float32),
            pltpu.VMEM((own, slots, blk), jnp.float32),
            sem, sem, sem, sem, sem, sem,
        ],
        compiler_params=pltpu.CompilerParams(
            collective_id=0, has_side_effects=True, vmem_limit_bytes=40 * 1024 * 1024
        ),
    )(ids, live, features, hot.astype(jnp.float32), scale)
    return jnp.log(weights) - jnp.log(phi.reshape(-1)) - jnp.log(beta.reshape(-1))


def solution(mesh):
    placed = (
        P(None, ("groups", "cells")),
        P(("groups", "cells")),
        P(("groups", "cells")),
        P(None, "cells"),
    )
    return jax.shard_map(
        local, mesh=mesh, in_specs=placed, out_specs=P(("groups", "cells")), check_vma=False
    )
```

time: 114 us -> 90.4 us (0.79)
  waiting for transfers between devices: 37.5 us -> 0 us
  Pallas kernels: 53.3 us -> 85.8 us
  starting transfers between devices: 7.86 us -> 0 us
  local copies, waits for them, and re-layouts: 10.8 us -> 2.96 us
  other arithmetic: 2.73 us -> 0.66 us
    ppermute x6 -> x0, waiting for transfers between devices: 37.5 us -> none  [from_next(): return lax.ppermute(block, 'cells', route)]
    pallas_call x2 -> x1, Pallas kernels: 53.3 us -> 85.8 us  [local(): pl.pallas_call(functools.partial(chain_kernel, slab, eps), in_specs=[smem...]
    ppermute x6 -> x0, starting transfers between devices: 7.86 us -> none  [from_next(): return lax.ppermute(block, 'cells', route)]
    unnamed x10 -> x8, local copies, waits for them, and re-layouts: 8.43 us -> 2.6 us
    slice x2 -> x0, local copies, waits for them, and re-layouts: 1.99 us -> none  [the longest x1 1.27 us: local(): above = from_next(features[:, :reach * blk], slab, 1)]
  transfers between devices with their start and end apart: 6 -> 0, of which waited for: 1 -> 0; matrix products, arithmetic and copies ran while one was open for 4% -> 0% of each run, Pallas kernels for 0% -> 0%
where the time goes in v3:
time: 90.4 us; the launch traced here: 89.4 us
  Pallas kernels  85.8 us (95%)
  local copies, waits for them, and re-layouts  2.96 us (3%)
    pallas_call x1, Pallas kernels, local(): pl.pallas_call(functools.partial(chain_kernel, slab, eps), in_specs=[smem...  85.8 us
    unnamed x8, local copies, waits for them, and re-layouts  2.6 us

profile of v3, /device:TPU:1, one launch (start us, length us, event | category | flops | bytes accessed | tf_op | source)
XLA Modules:
  0.0 89.4 jit_solution(17075325621708776400)
XLA Ops:
  0.0 0.0 copy-start.2
  0.0 0.7 copy-done.2
  0.7 0.1 copy.6
  0.8 0.1 gt.20
  0.9 0.1 copy.5
  1.0 0.1 eq.15
  1.1 0.0 copy-start.1
  1.1 0.7 copy-done.1
  1.8 0.0 copy-start
  1.8 1.2 %copy-done = f32[64,4096]{1,0:T(8,128)S(1)} copy-done((f32[64,4096]{1,0:T(8,128)S(1)}, f32[64,4096]{1,0:T(8,128)}, u32[]{:S(2)}) %copy-start) | copy-done | bytes 1048600
  3.0 0.0 copy-start.3
  3.0 85.8 %shard_map.46 = (f32[32,128]{1,0:T(8,128)S(1)}, f32[32,128]{1,0:T(8,128)S(1)}) custom-call(s32[8,32]{1,0:T(8,128)S(1)} %select_clamp_fusion.ids, f32[8,32]{1,0:T(8,128)S(1)} %get-tuple-element.10.live, f32[64,4096]{1,0:T(8,128)S(1)} %copy-done, f32[64,256]{1,0:T(8,128)S(1)} %fusion.1.hot, f32[32,128]{1,0:T(8,128)S(1)} %bitcast.11), custom_call_target="tpu_custom_call" | custom-call | tf_op jit(solution)/shard_map/pallas_call | solution.py:231
  88.8 0.0 copy-done.3
  88.8 0.6 bitcast_subtract_fusion
  (4 shorter events, 0.0 us)
Async XLA Ops:
  0.0 0.7 copy-start.2
  1.1 0.7 copy-start.1
  1.8 1.2 %copy-start = (f32[64,4096]{1,0:T(8,128)S(1)}, f32[64,4096]{1,0:T(8,128)}, u32[]{:S(2)}) copy-start(f32[64,4096]{1,0:T(8,128)} %feats.1) | copy-start | bytes 3145732
  3.0 85.8 %copy-start.3 = (f32[4096]{0:T(1024)S(1)}, f32[4096]{0:T(1024)}, u32[]{:S(2)}) copy-start(f32[4096]{0:T(1024)} %param.5) | copy-start | bytes 49156

commit v4 on v3

--- a/solution.py
+++ b/solution.py
@@ -35,7 +35,7 @@
 def chain_kernel(slab, eps, ids, live, feats, hot, scale, beta, phi,
                  tiles, fwin, stack,
                  window, vals, part, same_in, low_in, high_in, contrib,
-                 fsend, frecv, vsend, vrecv, psend, precv):
+                 fsend, frecv, rsend, rrecv, vsend, vrecv, psend, precv):
     me = lax.axis_index("cells")
     place, spot = me // slab, me % slab
     slots = ids.shape[0]
@@ -61,9 +61,16 @@
                     barrier, inc=1, device_id={"cells": me + step + o},
                     device_id_type=pl.DeviceIdType.MESH,
                 )
+    for o in (-1, 1):
+        @pl.when(inside[o + 1])
+        def _(o=o):
+            pl.semaphore_signal(
+                barrier, inc=1, device_id={"cells": me + o},
+                device_id_type=pl.DeviceIdType.MESH,
+            )
     sides = jnp.where(place > 0, 1, 0) + jnp.where(place < S - 1, 1, 0)
     near = 1 + jnp.where(inside[0], 1, 0) + jnp.where(inside[2], 1, 0)
-    pl.semaphore_wait(barrier, sides * near)
+    pl.semaphore_wait(barrier, sides * near + near - 1)
 
     def copy(src, dst, send, recv, target):
         return pltpu.make_async_remote_copy(
@@ -82,15 +89,18 @@
         1: (part.at[pl.ds(reach + own, reach)], high_in),
     }
 
-    feature_parts = {
-        -1: (feats.at[:, pl.ds(0, edge)], fwin.at[:, pl.ds(edge + middle, edge)]),
-        0: (feats, fwin.at[:, pl.ds(edge, middle)]),
-        1: (feats.at[:, pl.ds(middle - edge, edge)], fwin.at[:, pl.ds(0, edge)]),
-    }
-
-    def feature_copy(o):
-        src, dst = feature_parts[o]
-        return copy(src, dst, fsend.at[o + 1], frecv.at[o + 1], me - slab + o)
+    def feature_copy(h):
+        return copy(
+            feats.at[:, pl.ds(h * edge, edge)], fwin.at[:, pl.ds((h + 1) * edge, edge)],
+            fsend.at[h], frecv.at[h], me - slab,
+        )
+
+    def relay(h):
+        return copy(
+            fwin.at[:, pl.ds((h + 1) * edge, edge)],
+            fwin.at[:, pl.ds((1 - h) * (edge + middle), edge)],
+            rsend.at[h], rrecv.at[h], me + 2 * h - 1,
+        )
 
     def value_copy(o):
         src, dst = value_parts[o]
@@ -106,21 +116,43 @@
             def _(o=o):
                 getattr(make(o), act)()
 
-    each(place >= 1, feature_copy, "start")
+    @pl.when(place >= 1)
+    def _():
+        feature_copy(0).start()
+        feature_copy(1).start()
+
     each(place == S - 1, value_copy, "start")
     has_next = place < S - 1
-    each(has_next, feature_copy, "wait_recv", True)
 
     def lanes(b):
         return pl.ds(pl.multiple_of(b * blk, blk), blk)
 
+    def prepare(w, _):
+        stack[w] = stacked(fwin[:, lanes(w)], eps, False)
+        return 0
+
+    for h in (0, 1):
+        @pl.when(has_next)
+        def _(h=h):
+            feature_copy(h).wait_recv()
+
+        @pl.when(has_next & inside[2 * h])
+        def _(h=h):
+            relay(h).start()
+
+        @pl.when(has_next)
+        def _(h=h):
+            lax.fori_loop((h + 1) * reach, (h + 2) * reach, prepare, 0)
+
+    for h in (0, 1):
+        @pl.when(has_next & inside[2 - 2 * h])
+        def _(h=h):
+            relay(h).wait_recv()
+
     @pl.when(has_next)
     def _():
-        def prepare(w, _):
-            stack[w] = stacked(fwin[:, lanes(w)], eps, False)
-            return 0
-
-        lax.fori_loop(0, wide, prepare, 0)
+        lax.fori_loop(0, reach, prepare, 0)
+        lax.fori_loop(reach + own, wide, prepare, 0)
 
         def build(b, _):
             mine = stacked(feats[:, lanes(b)], eps, True).T
@@ -199,7 +231,17 @@
         phi[pl.ds(0, reach), :] += high_in[...]
 
     forward((place >= 1) & has_next)
-    each(place >= 1, feature_copy, "wait_send")
+
+    @pl.when(place >= 1)
+    def _():
+        feature_copy(0).wait_send()
+        feature_copy(1).wait_send()
+
+    for h in (0, 1):
+        @pl.when(has_next & inside[2 * h])
+        def _(h=h):
+            relay(h).wait_send()
+
     each(place >= 1, value_copy, "wait_send")
     each(has_next, sum_copy, "wait_send")
 
@@ -244,7 +286,7 @@
             pltpu.VMEM((reach, blk), jnp.float32),
             pltpu.VMEM((reach, blk), jnp.float32),
             pltpu.VMEM((own, slots, blk), jnp.float32),
-            sem, sem, sem, sem, sem, sem,
+            sem, sem, sem, sem, sem, sem, sem, sem,
         ],
         compiler_params=pltpu.CompilerParams(
             collective_id=0, has_side_effects=True, vmem_limit_bytes=40 * 1024 * 1024

time: 90.4 us -> 79.5 us (0.88)
  Pallas kernels: 85.8 us -> 74.9 us
    pallas_call x1, Pallas kernels: 85.8 us -> 74.9 us  [local(): pl.pallas_call(functools.partial(chain_kernel, slab, eps), in_specs=[smem...]
where the time goes in v4:
time: 79.5 us; the launch traced here: 78.6 us
  Pallas kernels  74.9 us (94%)
  local copies, waits for them, and re-layouts  2.96 us (4%)
    pallas_call x1, Pallas kernels, local(): pl.pallas_call(functools.partial(chain_kernel, slab, eps), in_specs=[smem...  74.9 us
    unnamed x8, local copies, waits for them, and re-layouts  2.6 us

profile of v4, /device:TPU:1, one launch (start us, length us, event | category | flops | bytes accessed | tf_op | source)
XLA Modules:
  0.0 78.6 jit_solution(9902057432880747728)
XLA Ops:
  0.0 0.0 copy-start.2
  0.0 0.7 copy-done.2
  0.7 0.1 copy.6
  0.8 0.1 gt.20
  0.9 0.1 copy.5
  1.0 0.1 eq.15
  1.1 0.0 copy-start.1
  1.1 0.7 copy-done.1
  1.8 0.0 copy-start
  1.8 1.2 %copy-done = f32[64,4096]{1,0:T(8,128)S(1)} copy-done((f32[64,4096]{1,0:T(8,128)S(1)}, f32[64,4096]{1,0:T(8,128)}, u32[]{:S(2)}) %copy-start) | copy-done | bytes 1048600
  3.0 0.0 copy-start.3
  3.0 74.9 %shard_map.46 = (f32[32,128]{1,0:T(8,128)S(1)}, f32[32,128]{1,0:T(8,128)S(1)}) custom-call(s32[8,32]{1,0:T(8,128)S(1)} %select_clamp_fusion.ids, f32[8,32]{1,0:T(8,128)S(1)} %get-tuple-element.10.live, f32[64,4096]{1,0:T(8,128)S(1)} %copy-done, f32[64,256]{1,0:T(8,128)S(1)} %fusion.1.hot, f32[32,128]{1,0:T(8,128)S(1)} %bitcast.11), custom_call_target="tpu_custom_call" | custom-call | tf_op jit(solution)/shard_map/pallas_call | solution.py:273
  78.0 0.0 copy-done.3
  78.0 0.6 bitcast_subtract_fusion
  (4 shorter events, 0.0 us)
Async XLA Ops:
  0.0 0.7 copy-start.2
  1.1 0.7 copy-start.1
  1.8 1.2 %copy-start = (f32[64,4096]{1,0:T(8,128)S(1)}, f32[64,4096]{1,0:T(8,128)}, u32[]{:S(2)}) copy-start(f32[64,4096]{1,0:T(8,128)} %feats.1) | copy-start | bytes 3145732
  3.0 74.9 %copy-start.3 = (f32[4096]{0:T(1024)S(1)}, f32[4096]{0:T(1024)}, u32[]{:S(2)}) copy-start(f32[4096]{0:T(1024)} %param.5) | copy-start | bytes 49156

commit v5 on v4

--- a/solution.py
+++ b/solution.py
@@ -30,6 +30,18 @@
     hi, lo = split(x * (2.0 * LOG2E / eps) if own else x)
     parts = [hi, lo, hi, tail] if own else [hi, hi, lo, tail]
     return jnp.concatenate(parts, axis=0)
+
+
+def blocks(low, high, body, at_once):
+    if (high - low) % at_once:
+        at_once = 1
+
+    def step(i, _):
+        for j in range(at_once):
+            body(low + i * at_once + j, 0)
+        return 0
+
+    lax.fori_loop(0, (high - low) // at_once, step, 0)
 
 
 def chain_kernel(slab, eps, ids, live, feats, hot, scale, beta, phi,
@@ -142,7 +154,7 @@
 
         @pl.when(has_next)
         def _(h=h):
-            lax.fori_loop((h + 1) * reach, (h + 2) * reach, prepare, 0)
+            blocks((h + 1) * reach, (h + 2) * reach, prepare, 2)
 
     for h in (0, 1):
         @pl.when(has_next & inside[2 - 2 * h])
@@ -151,8 +163,8 @@
 
     @pl.when(has_next)
     def _():
-        lax.fori_loop(0, reach, prepare, 0)
-        lax.fori_loop(reach + own, wide, prepare, 0)
+        blocks(0, reach, prepare, 2)
+        blocks(reach + own, wide, prepare, 2)
 
         def build(b, _):
             mine = stacked(feats[:, lanes(b)], eps, True).T
@@ -171,7 +183,7 @@
                     )
             return 0
 
-        lax.fori_loop(0, own, build, 0)
+        blocks(0, own, build, 2)
 
     def forward(cond):
         @pl.when(cond)
@@ -184,7 +196,7 @@
                     contrib[b, k : k + 1, :] = jnp.sum(out, axis=0, keepdims=True)
                 return 0
 
-            lax.fori_loop(0, own, fore, 0)
+            blocks(0, own, fore, 2)
             part[...] = lax.dot_general(
                 hot[...], contrib[...].reshape(own * slots, blk),
                 (((1,), (0,)), ((), ())),
@@ -218,7 +230,7 @@
             beta[pl.ds(b, 1), :] = rows[0:1]
             return 0
 
-        lax.fori_loop(0, own, back, 0)
+        blocks(0, own, back, 4)
         vals[...] = scale[...] * beta[...]
 
     each((place >= 1) & has_next, value_copy, "start")

time: 79.5 us -> 67.8 us (0.85)
  Pallas kernels: 74.9 us -> 62.9 us
    pallas_call x1, Pallas kernels: 74.9 us -> 62.9 us  [local(): pl.pallas_call(functools.partial(chain_kernel, slab, eps), in_specs=[smem...]
where the time goes in v5:
time: 67.8 us; the launch traced here: 66.6 us
  Pallas kernels  62.9 us (93%)
  local copies, waits for them, and re-layouts  2.96 us (4%)
    pallas_call x1, Pallas kernels, local(): pl.pallas_call(functools.partial(chain_kernel, slab, eps), in_specs=[smem...  62.9 us
    unnamed x8, local copies, waits for them, and re-layouts  2.6 us

profile of v5, /device:TPU:1, one launch (start us, length us, event | category | flops | bytes accessed | tf_op | source)
XLA Modules:
  0.0 66.6 jit_solution(11624535708752678609)
XLA Ops:
  0.0 0.0 copy-start.2
  0.0 0.7 %copy-done.2 = s32[8,32]{1,0:T(8,128)S(1)} copy-done((s32[8,32]{1,0:T(8,128)S(1)}, s32[8,32]{1,0:T(8,128)}, u32[]{:S(2)}) %copy-start.2) | copy-done | bytes 1048
  0.7 0.1 copy.6
  0.8 0.1 gt.20
  0.9 0.1 copy.5
  1.0 0.1 eq.15
  1.1 0.0 copy-start.1
  1.1 0.7 %copy-done.1 = f32[4096]{0:T(1024)S(1)} copy-done((f32[4096]{0:T(1024)S(1)}, f32[4096]{0:T(1024)}, u32[]{:S(2)}) %copy-start.1) | copy-done | bytes 16408
  1.8 0.0 copy-start
  1.8 1.2 %copy-done = f32[64,4096]{1,0:T(8,128)S(1)} copy-done((f32[64,4096]{1,0:T(8,128)S(1)}, f32[64,4096]{1,0:T(8,128)}, u32[]{:S(2)}) %copy-start) | copy-done | bytes 1048600
  3.0 0.0 copy-start.3
  3.0 62.9 %shard_map.46 = (f32[32,128]{1,0:T(8,128)S(1)}, f32[32,128]{1,0:T(8,128)S(1)}) custom-call(s32[8,32]{1,0:T(8,128)S(1)} %select_clamp_fusion.ids, f32[8,32]{1,0:T(8,128)S(1)} %get-tuple-element.10.live, f32[64,4096]{1,0:T(8,128)S(1)} %copy-done, f32[64,256]{1,0:T(8,128)S(1)} %fusion.1.hot, f32[32,128]{1,0:T(8,128)S(1)} %bitcast.11), custom_call_target="tpu_custom_call" | custom-call | tf_op jit(solution)/shard_map/pallas_call | solution.py:285
  65.9 0.0 copy-done.3
  65.9 0.6 bitcast_subtract_fusion
  (4 shorter events, 0.0 us)
Async XLA Ops:
  0.0 0.7 %copy-start.2 = (s32[8,32]{1,0:T(8,128)S(1)}, s32[8,32]{1,0:T(8,128)}, u32[]{:S(2)}) copy-start(s32[8,32]{1,0:T(8,128)} %param.7) | copy-start | bytes 3076
  1.1 0.7 %copy-start.1 = (f32[4096]{0:T(1024)S(1)}, f32[4096]{0:T(1024)}, u32[]{:S(2)}) copy-start(f32[4096]{0:T(1024)} %param.6) | copy-start | bytes 49156
  1.8 1.2 %copy-start = (f32[64,4096]{1,0:T(8,128)S(1)}, f32[64,4096]{1,0:T(8,128)}, u32[]{:S(2)}) copy-start(f32[64,4096]{1,0:T(8,128)} %feats.1) | copy-start | bytes 3145732
  3.0 62.9 %copy-start.3 = (f32[4096]{0:T(1024)S(1)}, f32[4096]{0:T(1024)}, u32[]{:S(2)}) copy-start(f32[4096]{0:T(1024)} %param.5) | copy-start | bytes 49156

commit v6 on v5

--- a/solution.py
+++ b/solution.py
@@ -101,17 +101,26 @@
         1: (part.at[pl.ds(reach + own, reach)], high_in),
     }
 
-    def feature_copy(h):
+    halves = 2 if reach % 2 == 0 else 1
+    pieces = 2 * halves
+    count = reach // halves
+    size = count * blk
+
+    def feature_copy(p):
         return copy(
-            feats.at[:, pl.ds(h * edge, edge)], fwin.at[:, pl.ds((h + 1) * edge, edge)],
-            fsend.at[h], frecv.at[h], me - slab,
+            feats.at[:, pl.ds(p * size, size)],
+            fwin.at[:, pl.ds(edge + p * size, size)],
+            fsend.at[p], frecv.at[p], me - slab,
         )
 
-    def relay(h):
+    def landing(p):
+        return p * size + edge + middle if p < halves else p * size - edge
+
+    def relay(p):
         return copy(
-            fwin.at[:, pl.ds((h + 1) * edge, edge)],
-            fwin.at[:, pl.ds((1 - h) * (edge + middle), edge)],
-            rsend.at[h], rrecv.at[h], me + 2 * h - 1,
+            fwin.at[:, pl.ds(edge + p * size, size)],
+            fwin.at[:, pl.ds(landing(p), size)],
+            rsend.at[p], rrecv.at[p], me - 1 if p < halves else me + 1,
         )
 
     def value_copy(o):
@@ -130,8 +139,8 @@
 
     @pl.when(place >= 1)
     def _():
-        feature_copy(0).start()
-        feature_copy(1).start()
+        for p in range(pieces):
+            feature_copy(p).start()
 
     each(place == S - 1, value_copy, "start")
     has_next = place < S - 1
@@ -143,29 +152,30 @@
         stack[w] = stacked(fwin[:, lanes(w)], eps, False)
         return 0
 
-    for h in (0, 1):
+    for p in range(pieces):
         @pl.when(has_next)
-        def _(h=h):
-            feature_copy(h).wait_recv()
-
-        @pl.when(has_next & inside[2 * h])
-        def _(h=h):
-            relay(h).start()
+        def _(p=p):
+            feature_copy(p).wait_recv()
+
+        @pl.when(has_next & inside[0 if p < halves else 2])
+        def _(p=p):
+            relay(p).start()
 
         @pl.when(has_next)
-        def _(h=h):
-            blocks((h + 1) * reach, (h + 2) * reach, prepare, 2)
-
-    for h in (0, 1):
-        @pl.when(has_next & inside[2 - 2 * h])
-        def _(h=h):
-            relay(h).wait_recv()
+        def _(p=p):
+            blocks(reach + p * count, reach + (p + 1) * count, prepare, 4)
+
+    for p in range(pieces):
+        @pl.when(has_next & inside[2 if p < halves else 0])
+        def _(p=p):
+            relay(p).wait_recv()
+
+        @pl.when(has_next)
+        def _(p=p):
+            blocks(landing(p) // blk, landing(p) // blk + count, prepare, 4)
 
     @pl.when(has_next)
     def _():
-        blocks(0, reach, prepare, 2)
-        blocks(reach + own, wide, prepare, 2)
-
         def build(b, _):
             mine = stacked(feats[:, lanes(b)], eps, True).T
             for k in range(0, slots, 2):
@@ -183,7 +193,7 @@
                     )
             return 0
 
-        blocks(0, own, build, 2)
+        blocks(0, own, build, 4)
 
     def forward(cond):
         @pl.when(cond)
@@ -196,7 +206,7 @@
                     contrib[b, k : k + 1, :] = jnp.sum(out, axis=0, keepdims=True)
                 return 0
 
-            blocks(0, own, fore, 2)
+            blocks(0, own, fore, 4)
             part[...] = lax.dot_general(
                 hot[...], contrib[...].reshape(own * slots, blk),
                 (((1,), (0,)), ((), ())),
@@ -246,13 +256,13 @@
 
     @pl.when(place >= 1)
     def _():
-        feature_copy(0).wait_send()
-        feature_copy(1).wait_send()
-
-    for h in (0, 1):
-        @pl.when(has_next & inside[2 * h])
-        def _(h=h):
-            relay(h).wait_send()
+        for p in range(pieces):
+            feature_copy(p).wait_send()
+
+    for p in range(pieces):
+        @pl.when(has_next & inside[0 if p < halves else 2])
+        def _(p=p):
+            relay(p).wait_send()
 
     each(place >= 1, value_copy, "wait_send")
     each(has_next, sum_copy, "wait_send")
@@ -281,7 +291,7 @@
     hot = (at == jnp.arange(wide, dtype=jnp.int32)[:, None]) & (
         live.T.reshape(1, own * slots) > 0
     )
-    sem = pltpu.SemaphoreType.DMA((3,))
+    sem = pltpu.SemaphoreType.DMA((4,))
     beta, phi = pl.pallas_call(
         functools.partial(chain_kernel, slab, eps),
         in_specs=[smem] * 2 + [vmem] * 3,

time: 67.8 us -> 62 us (0.914); the launches traced: 66.6 us -> 61.7 us
  Pallas kernels: 62.9 us -> 58.1 us
    pallas_call x1, Pallas kernels: 62.9 us -> 58.1 us  [local(): pl.pallas_call(functools.partial(chain_kernel, slab, eps), in_specs=[smem...]
where the time goes in v6:
time: 62 us; the launch traced here: 61.7 us
  Pallas kernels  58.1 us (94%)
  local copies, waits for them, and re-layouts  2.96 us (5%)
  other arithmetic  0.66 us (1%)
    pallas_call x1, Pallas kernels, local(): pl.pallas_call(functools.partial(chain_kernel, slab, eps), in_specs=[smem...  58.1 us
    unnamed x8, local copies, waits for them, and re-layouts  2.6 us

profile of v6, /device:TPU:1, one launch (start us, length us, event | category | flops | bytes accessed | tf_op | source)
XLA Modules:
  0.0 61.7 jit_solution(9855598543836604930)
XLA Ops:
  0.0 0.0 copy-start.2
  0.0 0.7 %copy-done.2 = s32[8,32]{1,0:T(8,128)S(1)} copy-done((s32[8,32]{1,0:T(8,128)S(1)}, s32[8,32]{1,0:T(8,128)}, u32[]{:S(2)}) %copy-start.2) | copy-done | bytes 1048
  0.7 0.1 copy.6
  0.8 0.1 gt.20
  0.9 0.1 copy.5
  1.0 0.1 eq.15
  1.1 0.0 copy-start.1
  1.1 0.7 %copy-done.1 = f32[4096]{0:T(1024)S(1)} copy-done((f32[4096]{0:T(1024)S(1)}, f32[4096]{0:T(1024)}, u32[]{:S(2)}) %copy-start.1) | copy-done | bytes 16408
  1.8 0.0 copy-start
  1.8 1.2 %copy-done = f32[64,4096]{1,0:T(8,128)S(1)} copy-done((f32[64,4096]{1,0:T(8,128)S(1)}, f32[64,4096]{1,0:T(8,128)}, u32[]{:S(2)}) %copy-start) | copy-done | bytes 1048600
  3.0 0.0 copy-start.3
  3.0 58.1 %shard_map.46 = (f32[32,128]{1,0:T(8,128)S(1)}, f32[32,128]{1,0:T(8,128)S(1)}) custom-call(s32[8,32]{1,0:T(8,128)S(1)} %select_clamp_fusion.ids, f32[8,32]{1,0:T(8,128)S(1)} %get-tuple-element.10.live, f32[64,4096]{1,0:T(8,128)S(1)} %copy-done, f32[64,256]{1,0:T(8,128)S(1)} %fusion.1.hot, f32[32,128]{1,0:T(8,128)S(1)} %bitcast.11), custom_call_target="tpu_custom_call" | custom-call | tf_op jit(solution)/shard_map/pallas_call | solution.py:295
  61.1 0.0 copy-done.3
  61.1 0.6 %bitcast_subtract_fusion = f32[4096]{0:T(1024)} fusion(f32[32,128]{1,0:T(8,128)S(1)} %get-tuple-element.8, f32[32,128]{1,0:T(8,128)S(1)} %get-tuple-element.7, f32[4096]{0:T(1024)S(1)} %copy-done.3), kind=kLoop, calls=%fused_computation.3 | loop fusion | flops 8192 | bytes 65536 | tf_op jit(solution)/shard_map/sub | solution.py:317
  (4 shorter events, 0.0 us)
Async XLA Ops:
  0.0 0.7 %copy-start.2 = (s32[8,32]{1,0:T(8,128)S(1)}, s32[8,32]{1,0:T(8,128)}, u32[]{:S(2)}) copy-start(s32[8,32]{1,0:T(8,128)} %param.7) | copy-start | bytes 3076
  1.1 0.7 %copy-start.1 = (f32[4096]{0:T(1024)S(1)}, f32[4096]{0:T(1024)}, u32[]{:S(2)}) copy-start(f32[4096]{0:T(1024)} %param.6) | copy-start | bytes 49156
  1.8 1.2 %copy-start = (f32[64,4096]{1,0:T(8,128)S(1)}, f32[64,4096]{1,0:T(8,128)}, u32[]{:S(2)}) copy-start(f32[64,4096]{1,0:T(8,128)} %feats.1) | copy-start | bytes 3145732
  3.0 58.1 %copy-start.3 = (f32[4096]{0:T(1024)S(1)}, f32[4096]{0:T(1024)}, u32[]{:S(2)}) copy-start(f32[4096]{0:T(1024)} %param.5) | copy-start | bytes 49156

commit v7 on v6

--- a/solution.py
+++ b/solution.py
@@ -101,7 +101,7 @@
         1: (part.at[pl.ds(reach + own, reach)], high_in),
     }
 
-    halves = 2 if reach % 2 == 0 else 1
+    halves = 4 if reach % 4 == 0 else 1
     pieces = 2 * halves
     count = reach // halves
     size = count * blk
@@ -193,7 +193,7 @@
                     )
             return 0
 
-        blocks(0, own, build, 4)
+        blocks(0, own, build, 8)
 
     def forward(cond):
         @pl.when(cond)
@@ -206,7 +206,7 @@
                     contrib[b, k : k + 1, :] = jnp.sum(out, axis=0, keepdims=True)
                 return 0
 
-            blocks(0, own, fore, 4)
+            blocks(0, own, fore, 8)
             part[...] = lax.dot_general(
                 hot[...], contrib[...].reshape(own * slots, blk),
                 (((1,), (0,)), ((), ())),
@@ -240,7 +240,7 @@
             beta[pl.ds(b, 1), :] = rows[0:1]
             return 0
 
-        blocks(0, own, back, 4)
+        blocks(0, own, back, 8)
         vals[...] = scale[...] * beta[...]
 
     each((place >= 1) & has_next, value_copy, "start")
@@ -291,7 +291,7 @@
     hot = (at == jnp.arange(wide, dtype=jnp.int32)[:, None]) & (
         live.T.reshape(1, own * slots) > 0
     )
-    sem = pltpu.SemaphoreType.DMA((4,))
+    sem = pltpu.SemaphoreType.DMA((8,))
     beta, phi = pl.pallas_call(
         functools.partial(chain_kernel, slab, eps),
         in_specs=[smem] * 2 + [vmem] * 3,

time: 62 us -> 58.1 us (0.937)
  Pallas kernels: 58.1 us -> 54.1 us
    pallas_call x1, Pallas kernels: 58.1 us -> 54.1 us  [local(): pl.pallas_call(functools.partial(chain_kernel, slab, eps), in_specs=[smem...]
where the time goes in v7:
time: 58.1 us; the launch traced here: 57.8 us
  Pallas kernels  54.1 us (93%)
  local copies, waits for them, and re-layouts  2.96 us (5%)
  other arithmetic  0.66 us (1%)
    pallas_call x1, Pallas kernels, local(): pl.pallas_call(functools.partial(chain_kernel, slab, eps), in_specs=[smem...  54.1 us
    unnamed x8, local copies, waits for them, and re-layouts  2.6 us

profile of v7, /device:TPU:1, one launch (start us, length us, event | category | flops | bytes accessed | tf_op | source)
XLA Modules:
  0.0 57.8 jit_solution(11284285112402361906)
XLA Ops:
  0.0 0.0 copy-start.2
  0.0 0.7 %copy-done.2 = s32[8,32]{1,0:T(8,128)S(1)} copy-done((s32[8,32]{1,0:T(8,128)S(1)}, s32[8,32]{1,0:T(8,128)}, u32[]{:S(2)}) %copy-start.2) | copy-done | bytes 1048
  0.7 0.1 copy.6
  0.8 0.1 gt.20
  0.9 0.1 copy.5
  1.0 0.1 eq.15
  1.1 0.0 copy-start.1
  1.1 0.7 %copy-done.1 = f32[4096]{0:T(1024)S(1)} copy-done((f32[4096]{0:T(1024)S(1)}, f32[4096]{0:T(1024)}, u32[]{:S(2)}) %copy-start.1) | copy-done | bytes 16408
  1.8 0.0 copy-start
  1.8 1.2 %copy-done = f32[64,4096]{1,0:T(8,128)S(1)} copy-done((f32[64,4096]{1,0:T(8,128)S(1)}, f32[64,4096]{1,0:T(8,128)}, u32[]{:S(2)}) %copy-start) | copy-done | bytes 1048600
  3.0 0.0 copy-start.3
  3.0 54.1 %shard_map.46 = (f32[32,128]{1,0:T(8,128)S(1)}, f32[32,128]{1,0:T(8,128)S(1)}) custom-call(s32[8,32]{1,0:T(8,128)S(1)} %select_clamp_fusion.ids, f32[8,32]{1,0:T(8,128)S(1)} %get-tuple-element.10.live, f32[64,4096]{1,0:T(8,128)S(1)} %copy-done, f32[64,256]{1,0:T(8,128)S(1)} %fusion.1.hot, f32[32,128]{1,0:T(8,128)S(1)} %bitcast.11), custom_call_target="tpu_custom_call" | custom-call | tf_op jit(solution)/shard_map/pallas_call | solution.py:295
  57.1 0.0 copy-done.3
  57.2 0.6 %bitcast_subtract_fusion = f32[4096]{0:T(1024)} fusion(f32[32,128]{1,0:T(8,128)S(1)} %get-tuple-element.8, f32[32,128]{1,0:T(8,128)S(1)} %get-tuple-element.7, f32[4096]{0:T(1024)S(1)} %copy-done.3), kind=kLoop, calls=%fused_computation.3 | loop fusion | flops 8192 | bytes 65536 | tf_op jit(solution)/shard_map/sub | solution.py:317
  (4 shorter events, 0.0 us)
Async XLA Ops:
  0.0 0.7 %copy-start.2 = (s32[8,32]{1,0:T(8,128)S(1)}, s32[8,32]{1,0:T(8,128)}, u32[]{:S(2)}) copy-start(s32[8,32]{1,0:T(8,128)} %param.7) | copy-start | bytes 3076
  1.1 0.7 %copy-start.1 = (f32[4096]{0:T(1024)S(1)}, f32[4096]{0:T(1024)}, u32[]{:S(2)}) copy-start(f32[4096]{0:T(1024)} %param.6) | copy-start | bytes 49156
  1.8 1.2 %copy-start = (f32[64,4096]{1,0:T(8,128)S(1)}, f32[64,4096]{1,0:T(8,128)}, u32[]{:S(2)}) copy-start(f32[64,4096]{1,0:T(8,128)} %feats.1) | copy-start | bytes 3145732
  3.0 54.1 %copy-start.3 = (f32[4096]{0:T(1024)S(1)}, f32[4096]{0:T(1024)}, u32[]{:S(2)}) copy-start(f32[4096]{0:T(1024)} %param.5) | copy-start | bytes 49156
